TPU v7x, 32 devices: a whole 2x2x4 slice. The times are simulated.
32 devices in a mesh: span: 4 (over y, x), seq: 2 (over core), mp: 4 (over z).
Axes of the slice: x: 2, y: 2, z: 4, core: 2. Of those that a mesh axis runs over, the one named last changes fastest.
Arguments:
- queries: bfloat16 [4, 128, 6144], P('span', 'seq', 'mp'), may hold values from -30 to 30
- keys: bfloat16 [4, 128, 1024], P('span', 'seq'), may hold values from -30 to 30
- values: bfloat16 [4, 128, 1024], P('span', 'seq'), may hold values from -6 to 6
- clip_ids: int32 [128], P('seq'), may hold values from 0 to 5, never falling along the last dimension, each value on 1 to 64 neighbouring positions
- block_mask: int32 [4, 4], replicated, may hold values from 0 to 1, as said below
- out_weight: bfloat16 [6144, 6144], P('mp'), may hold values from -0.078125 to 0.078125
Outputs:
- projected: bfloat16 [4, 128, 6144], P('span', 'seq', 'mp')
Inputs may be any that keep to these rules, and one draw needn't show every extreme that they name: block_mask[c][c] is 1; block_mask[c][c2] is 0 unless c - 3 < c2 <= c. `clip_ids`: clip ids never fall along the rows; each clip has 1 to 64 rows, one exactly that many.
All inputs are finite; a program needn't handle non-finite values.
Results may differ from a plain program's by a relative error of at most 0.017.
Values may be sent and summed in bfloat16 or wider, within the bound.
A program may use at most 64 MiB of HBM per device.

v0:
```python
import jax
import jax.numpy as jnp
from jax import lax
from jax.sharding import PartitionSpec as P

HEAD_DIM = 128
WINDOW = 3
GROUP = 6


def passed_along(x, axis, by):
    size = lax.axis_size(axis)
    pairs = [(i, i + by) for i in range(size) if 0 <= i + by < size]
    return lax.ppermute(x, axis, pairs)


def on_device(queries, keys, values, clip_ids, block_mask, out_weight):
    row_count = queries.shape[1]
    local_width = queries.shape[2]
    head_count = local_width // HEAD_DIM
    kv_width = keys.shape[2]
    kv_count = kv_width // HEAD_DIM
    score_scale = HEAD_DIM ** (-0.5)
    span_index = lax.axis_index("span")
    first_head = lax.axis_index("mp") * head_count
    kv_choice = (first_head + jnp.arange(head_count, dtype=jnp.int32)) // GROUP
    packed = jnp.concatenate([keys, values], axis=2)
    query_heads = jnp.transpose(queries[0].reshape(row_count, head_count, HEAD_DIM), (1, 0, 2))
    mask_row = lax.dynamic_index_in_dim(block_mask, span_index, 0, keepdims=False)
    visible = []
    for j in range(WINDOW):
        earlier = span_index - j
        entry = lax.dynamic_index_in_dim(mask_row, jnp.maximum(earlier, 0), 0, keepdims=False)
        visible.append(jnp.where(earlier >= 0, entry, 0))
    initial = (
        jnp.full((head_count, row_count), -1e30, jnp.float32),
        jnp.zeros((head_count, row_count), jnp.float32),
        jnp.zeros((head_count, row_count, HEAD_DIM), jnp.float32),
    )
    stacked = [packed[0]]
    for j in range(1, WINDOW):
        stacked.append(passed_along(packed[0], "span", j))
    running_max, running_total, running_acc = initial
    blocks = lax.all_gather(jnp.stack(stacked, axis=0), "seq", axis=1, tiled=True)
    key_clips = lax.all_gather(clip_ids[None, :], "seq", axis=1, tiled=True)
    piece_rows = blocks.shape[1]
    for j in range(WINDOW):
        key_all = blocks[j, :, :kv_width].reshape(piece_rows, kv_count, HEAD_DIM)
        value_all = blocks[j, :, kv_width:].reshape(piece_rows, kv_count, HEAD_DIM)
        key_block = jnp.take(key_all, kv_choice, axis=1)
        value_block = jnp.take(value_all, kv_choice, axis=1)
        s = (
            jnp.einsum("hqd,khd->hqk", query_heads, key_block, preferred_element_type=jnp.float32)
            * score_scale
        )
        allowed = (visible[j] == 1) & (clip_ids[:, None] == key_clips[0][None, :])
        s = jnp.where(allowed[None], s, -jnp.inf)
        new_max = jnp.maximum(running_max, jnp.max(s, axis=2))
        p = jnp.exp(s - new_max[:, :, None])
        factor = jnp.exp(running_max - new_max)
        running_total = running_total * factor + jnp.sum(p, axis=2)
        running_acc = running_acc * factor[:, :, None] + jnp.einsum(
            "hqk,khd->hqd", p.astype(jnp.bfloat16), value_block, preferred_element_type=jnp.float32
        )
        running_max = new_max
    result = (running_max, running_total, running_acc)
    final_max, final_total, final_acc = result
    attended = final_acc / final_total[:, :, None]
    attended = (
        jnp.transpose(attended, (1, 0, 2)).reshape(row_count, local_width).astype(jnp.bfloat16)
    )
    partial_sum = jnp.dot(attended, out_weight, preferred_element_type=jnp.float32)[None]
    return lax.psum_scatter(partial_sum.astype(jnp.bfloat16), "mp", scatter_dimension=2, tiled=True)


def solution(mesh):
    in_specs = (
        P("span", "seq", "mp"),
        P("span", "seq", None),
        P("span", "seq", None),
        P("seq"),
        P(),
        P("mp", None),
    )
    out_specs = P("span", "seq", "mp")
    return jax.shard_map(
        on_device, mesh=mesh, in_specs=in_specs, out_specs=out_specs, check_vma=False
    )
```

profile of v0, /device:TPU:0, one launch (start us, length us, event | category | flops | bytes accessed | tf_op | source)
XLA Modules:
  0.0 90.0 jit_solution(772528283099189083)
XLA Ops:
  6.5 0.9 %constant_dynamic-update-slice_fusion.1 = bf16[1,64,2048]{2,1,0:T(8,128)(2,1)S(1)} fusion(bf16[1,64,1024]{2,1,0:T(8,128)(2,1)} %param.9), kind=kLoop, calls=%fused_computation.88 | loop fusion | bytes 262144
  7.5 0.9 %constant_dynamic-update-slice_fusion = bf16[1,64,2048]{2,1,0:T(8,128)(2,1)S(1)} fusion(bf16[1,64,2048]{2,1,0:T(8,128)(2,1)S(1)} %constant_dynamic-update-slice_fusion.1, bf16[1,64,1024]{2,1,0:T(8,128)(2,1)} %param.10), kind=kLoop, calls=%fused_computation.87 | loop fusion | bytes 262144 | tf_op jit(solution)/shard_map/concatenate | solution.py:27
  8.4 4.9 %collective-permute-start.1 = (bf16[64,2048]{1,0:T(8,128)(2,1)S(1)}, bf16[64,2048]{1,0:T(8,128)(2,1)S(1)}, u32[]{:S(2)}, u32[]{:S(2)}) collective-permute-start(bf16[64,2048]{1,0:T(8,128)(2,1)S(1)} %bitcast.131), channel_id=1, source_target_pairs={{0,16},{8,24},{1,17},{9,25},{2,18},{10,26},{3,19},{11,27},{4,20},{... | collective-permute-start | bytes 786440 | tf_op jit(solution)/shard_map/ppermute | solution.py:14
  13.3 3.4 %collective-permute-start = (bf16[64,2048]{1,0:T(8,128)(2,1)S(1)}, bf16[64,2048]{1,0:T(8,128)(2,1)S(1)}, u32[]{:S(2)}, u32[]{:S(2)}) collective-permute-start(bf16[64,2048]{1,0:T(8,128)(2,1)S(1)} %bitcast.132), channel_id=1, source_target_pairs={{0,8},{8,16},{16,24},{1,9},{9,17},{17,25},{2,10},{10,18},{18,26},{... | collective-permute-start | bytes 786440 | tf_op jit(solution)/shard_map/ppermute | solution.py:14
  16.7 7.7 %collective-permute-done.1 = bf16[64,2048]{1,0:T(8,128)(2,1)S(1)} collective-permute-done((bf16[64,2048]{1,0:T(8,128)(2,1)S(1)}, bf16[64,2048]{1,0:T(8,128)(2,1)S(1)}, u32[]{:S(2)}, u32[]{:S(2)}) %collective-permute-start.1) | collective-permute-done | bytes 262176 | tf_op jit(solution)/shard_map/ppermute | solution.py:14
  24.4 1.0 %pad_maximum_fusion = bf16[3,64,2048]{2,1,0:T(8,128)(2,1)} fusion(bf16[1,64,2048]{2,1,0:T(8,128)(2,1)S(1)} %bitcast.136, bf16[1,64,2048]{2,1,0:T(8,128)(2,1)S(1)} %bitcast.137, bf16[1,64,2048]{2,1,0:T(8,128)(2,1)S(1)} %constant_dynamic-update-slice_fusion), kind=kLoop, calls=%fused_computation.28 | loop fusion | flops 786432 | bytes 1572864 | tf_op jit(solution)/shard_map/stack | solution.py:44
  25.5 1.1 %reshape_squeeze.22 = bf16[64,12,128]{2,1,0:T(8,128)(2,1)S(1)} reshape(bf16[1,64,1536]{2,1,0:T(8,128)(2,1)} %param.8) | data formatting | bytes 393216 | tf_op jit(solution)/shard_map/reshape;squeeze | solution.py:28
  26.6 1.4 %fusion.73 = (s32[1,1]{1,0:T(1,128)}, s32[1,1]{1,0:T(1,128)}, s32[1,1]{1,0:T(1,128)}) fusion(s32[4,4]{1,0:T(4,128)} %param.12, s32[]{:T(128)S(6)} %select_n.42, s32[]{:T(128)S(6)} %max.63, s32[]{:T(128)S(6)} %max.57, s32[]{:T(128)S(6)} %max.59), kind=kLoop, calls=%fused_computation.102 | loop fusion | bytes 40 | tf_op jit(solution)/shard_map/jit(dynamic_index_in_dim)/dynamic_slice | solution.py:33
  29.9 1.2 %dynamic-slice.3 = u32[1]{0:T(128)} dynamic-slice(u32[32]{0:T(128)} %constant.101, u32[]{:T(128)S(6)} %add.78), dynamic_slice_sizes={1} | dynamic-slice | bytes 12
  31.8 0.9 dynamic-update-slice
  32.6 1.8 %all-reduce = s32[128]{0:T(128)S(1)} all-reduce(s32[128]{0:T(128)S(1)} %dynamic-update-slice), channel_id=2, replica_groups=mesh['span'=4,'seq'=2,'mp'=4] {'seq'}, use_global_device_ids=true, to_apply=%add | all-reduce | flops 128 | bytes 1024
  34.5 0.7 compare_and_fusion
  35.2 1.4 %all-gather.3.cloned.1.call-done = bf16[3,128,2048]{2,1,0:T(8,128)(2,1)} async-done(((bf16[3,64,2048]{2,1,0:T(8,128)(2,1)}), bf16[3,128,2048]{2,1,0:T(8,128)(2,1)}) %all-gather.3.cloned.1.call-update) | async-done | bytes 1572880 | tf_op jit(solution)/shard_map/all_gather | solution.py:44
  36.7 1.5 %fusion.72 = (bf16[1,128,1024]{2,1,0:T(8,128)(2,1)S(1)}, bf16[1,128,1024]{2,1,0:T(8,128)(2,1)S(1)}, bf16[1,128,1024]{2,1,0:T(8,128)(2,1)S(1)}, bf16[1,128,1024]{...) fusion(bf16[3,128,2048]{2,1,0:T(8,128)(2,1)} %all-gather.3.cloned.1.call-done), kind=kLoop, calls=%fused_computation.101 | loop fusion | bytes 3145728 | tf_op jit(solution)/shard_map/slice | solution.py:49
  38.9 0.6 gather_fusion.1
  39.5 0.6 gather_fusion
  40.5 0.6 gather_fusion.4
  41.5 0.6 gather_fusion.2
  42.5 0.6 gather_fusion.3
  43.5 0.6 gather_fusion.5
  44.1 0.5 fusion.76
  46.6 0.6 fusion.12
  47.9 10.6 %fusion = bf16[1,64,6144]{2,1,0:T(8,128)(2,1)} fusion(bf16[1536,6144]{1,0:T(8,128)(2,1)} %param.13, bf16[12,8,8,128]{3,2,1,0:T(8,128)(2,1)S(1)} %fusion.14), kind=kOutput, calls=%fused_computation.7 | convolution fusion | flops 1208352768 | bytes 19857408 | tf_op jit(solution)/shard_map/dot_general | solution.py:72
  58.5 24.6 %reduce-scatter.2.cloned.1.call-done = bf16[1,64,1536]{2,1,0:T(8,128)(2,1)} async-done(((bf16[1,64,6144]{2,1,0:T(8,128)(2,1)}), bf16[1,64,1536]{2,1,0:T(8,128)(2,1)}) %reduce-scatter.2.cloned.1.call-update) | async-done | bytes 196624 | tf_op jit(solution)/shard_map/reduce_scatter | solution.py:73
  (29 shorter events, 4.8 us)
Async XLA Ops:
  6.5 30.1 %all-gather.3.cloned.1.call-start = ((), (), s32[]{:S(2)}) async-start(), calls=%async_computation.1 | async-start | bytes 2359296 | tf_op jit(solution)/shard_map/all_gather | solution.py:44
  8.4 16.0 %collective-permute-start.1 = (bf16[64,2048]{1,0:T(8,128)(2,1)S(1)}, bf16[64,2048]{1,0:T(8,128)(2,1)S(1)}, u32[]{:S(2)}, u32[]{:S(2)}) collective-permute-start(bf16[64,2048]{1,0:T(8,128)(2,1)S(1)} %bitcast.131), channel_id=1, source_target_pairs={{0,16},{8,24},{1,17},{9,25},{2,18},{10,26},{3,19},{11,27},{4,20},{... | collective-permute-start | bytes 786440 | tf_op jit(solution)/shard_map/ppermute | solution.py:14
  13.3 11.2 %collective-permute-start = (bf16[64,2048]{1,0:T(8,128)(2,1)S(1)}, bf16[64,2048]{1,0:T(8,128)(2,1)S(1)}, u32[]{:S(2)}, u32[]{:S(2)}) collective-permute-start(bf16[64,2048]{1,0:T(8,128)(2,1)S(1)} %bitcast.132), channel_id=1, source_target_pairs={{0,8},{8,16},{16,24},{1,9},{9,17},{17,25},{2,10},{10,18},{18,26},{... | collective-permute-start | bytes 786440 | tf_op jit(solution)/shard_map/ppermute | solution.py:14
  25.4 57.7 %reduce-scatter.2.cloned.1.call-start = ((), (), s32[]{:S(2)}) async-start(), calls=%async_computation.2 | async-start | bytes 983040 | tf_op jit(solution)/shard_map/reduce_scatter | solution.py:73
Sparse Core Ops, SparseCore 0:
  25.5 11.0 all-gather.2
  58.7 24.4 reduce-scatter.1
where the time goes:
time: 90.3 us; the launch traced here: 90 us
  waiting for transfers between devices  33.8 us (37%)
  between operations  16.2 us (18%)
  local copies, waits for them, and re-layouts  13.7 us (15%)
  matrix products  13.4 us (15%)
  starting transfers between devices  8.34 us (9%)
  other arithmetic  2.64 us (3%)
  blocking collectives  1.81 us (2%)
    reduce_scatter x1, waiting for transfers between devices, on_device(): lax.psum_scatter(partial_sum.astype(jnp.bfloat16), 'mp', scatter_dimensio...  24.6 us
    dot_general x1, matrix products, on_device(): jnp.dot(attended, out_weight, preferred_element_type=jnp.float32)[None]  10.6 us
    ppermute x2, starting transfers between devices, passed_along(): return lax.ppermute(x, axis, pairs)  8.3 us
    ppermute x2, waiting for transfers between devices, passed_along(): return lax.ppermute(x, axis, pairs)  7.73 us
    unnamed x10, local copies, waits for them, and re-layouts  4.03 us
    gather x3, local copies, waits for them, and re-layouts, on_device(): value_block = jnp.take(value_all, kv_choice, axis=1)  1.88 us
    gather x3, local copies, waits for them, and re-layouts, on_device(): key_block = jnp.take(key_all, kv_choice, axis=1)  1.87 us
    unnamed x1, blocking collectives  1.81 us
  transfers between devices with their start and end apart: 4, of which 3 were waited for; matrix products, arithmetic and copies ran while one was open for 6% of the time, Pallas kernels for 0%

commit v1 on v0

v1 whole, which is shorter than its diff:
```python
import functools
import jax
import jax.numpy as jnp
from jax import lax
from jax.experimental import pallas as pl
from jax.experimental.pallas import tpu as pltpu
from jax.sharding import PartitionSpec as P

HEAD_DIM = 128
WINDOW = 3
GROUP = 6
MASKED = -1e30
MESH = pl.DeviceIdType.MESH


def kernel(
    spans, seqs, n, pieces, kv_count, kv_total,
    q_ref, k_ref, v_ref, clip_ref, mask_ref, w_ref, out_ref,
    qbuf, kbuf, vbuf, own_clip, clips, wbuf, att, part, sendbuf, recvbuf, outbuf,
    local_sem, w_sem, span_send, seq_send, kv_recv, clip_send, clip_recv, sum_send, sum_recv, out_sem,
):
    rows, local_width = qbuf.shape
    head_count = local_width // HEAD_DIM
    width = wbuf.shape[2]
    chunk = width * pieces
    kv_width = kv_count * HEAD_DIM
    steps = n * pieces
    c = lax.axis_index("span")
    s = lax.axis_index("seq")
    me = lax.axis_index("mp")

    first_kv = jnp.minimum(me * head_count // GROUP, kv_total - kv_count)
    kv_columns = pl.ds(pl.multiple_of(first_kv * HEAD_DIM, HEAD_DIM), kv_width)

    local = [
        pltpu.make_async_copy(k_ref.at[0, :, kv_columns], kbuf.at[0, s], local_sem.at[0]),
        pltpu.make_async_copy(v_ref.at[0, :, kv_columns], vbuf.at[0, s], local_sem.at[1]),
        pltpu.make_async_copy(clip_ref, own_clip, local_sem.at[2]),
        pltpu.make_async_copy(q_ref.at[0], qbuf, local_sem.at[3]),
    ]
    for copy in local:
        copy.start()

    turn = 2 * (2 * me // n) - 1

    def chunk_at(step):
        return lax.rem(me + turn * (step + 1) + 2 * n, n)

    def w_copy(i):
        start = chunk_at(i // pieces) * chunk + lax.rem(i, pieces) * width
        return pltpu.make_async_copy(
            w_ref.at[:, pl.ds(pl.multiple_of(start, HEAD_DIM), width)], wbuf.at[i], w_sem.at[i]
        )

    barrier = pltpu.get_barrier_semaphore()
    for j in range(1, WINDOW):
        @pl.when(c >= j)
        def _():
            pl.semaphore_signal(barrier, inc=1, device_id={"span": c - j}, device_id_type=MESH)
    for d in range(1, seqs):
        pl.semaphore_signal(
            barrier, inc=1, device_id={"seq": lax.rem(s + d, seqs)}, device_id_type=MESH
        )

    @pl.when(me > 0)
    def _():
        pl.semaphore_signal(barrier, inc=1, device_id={"mp": me - 1}, device_id_type=MESH)

    @pl.when(me < n - 1)
    def _():
        pl.semaphore_signal(barrier, inc=1, device_id={"mp": me + 1}, device_id_type=MESH)

    def start_w(i, carry):
        w_copy(i).start()
        return carry

    lax.fori_loop(0, steps, start_w, 0)

    for j in range(1, WINDOW):
        @pl.when(c < j)
        def _():
            kbuf[j] = jnp.zeros(kbuf.shape[1:], kbuf.dtype)
            vbuf[j] = jnp.zeros(vbuf.shape[1:], vbuf.dtype)

    local[2].wait()
    clips[s] = jnp.broadcast_to(own_clip[...], clips.shape[1:])
    local[0].wait()
    local[1].wait()
    later_spans = jnp.minimum(spans - 1 - c, WINDOW - 1)
    z_neighbours = jnp.minimum(me, 1) + jnp.minimum(n - 1 - me, 1)
    pl.semaphore_wait(barrier, seqs - 1 + later_spans + z_neighbours)

    bufs = (kbuf, vbuf)

    def to_span(j, a):
        return pltpu.make_async_remote_copy(
            src_ref=bufs[a].at[0, s],
            dst_ref=bufs[a].at[j, s],
            send_sem=span_send.at[j, a],
            recv_sem=kv_recv.at[j, s, a],
            device_id={"span": c + j},
            device_id_type=MESH,
        )

    def to_seq(j, d, a):
        return pltpu.make_async_remote_copy(
            src_ref=bufs[a].at[j, s],
            dst_ref=bufs[a].at[j, s],
            send_sem=seq_send.at[j, d, a],
            recv_sem=kv_recv.at[j, s, a],
            device_id={"seq": lax.rem(s + d, seqs)},
            device_id_type=MESH,
        )

    def arrival(j, s2, a):
        return pltpu.make_async_remote_copy(
            src_ref=bufs[a].at[j, s2],
            dst_ref=bufs[a].at[j, s2],
            send_sem=seq_send.at[0, 0, a],
            recv_sem=kv_recv.at[j, s2, a],
            device_id={"seq": s2},
            device_id_type=MESH,
        )

    def clip_copy(d, source):
        return pltpu.make_async_remote_copy(
            src_ref=clips.at[source],
            dst_ref=clips.at[source],
            send_sem=clip_send.at[d],
            recv_sem=clip_recv.at[source],
            device_id={"seq": lax.rem(s + d, seqs)},
            device_id_type=MESH,
        )

    for a in range(2):
        for j in range(WINDOW - 1, 0, -1):
            @pl.when(c + j < spans)
            def _():
                to_span(j, a).start()
    for d in range(1, seqs):
        clip_copy(d, s).start()
    for a in range(2):
        for d in range(1, seqs):
            to_seq(0, d, a).start()

    def relay(a):
        for j in range(1, WINDOW):
            @pl.when(c >= j)
            def _():
                arrival(j, s, a).wait_recv()
                for d in range(1, seqs):
                    to_seq(j, d, a).start()

    def await_others(a):
        for d in range(1, seqs):
            arrival(0, lax.rem(s + d, seqs), a).wait_recv()
        for j in range(1, WINDOW):
            @pl.when(c >= j)
            def _():
                for d in range(1, seqs):
                    arrival(j, lax.rem(s + d, seqs), a).wait_recv()

    for d in range(1, seqs):
        clip_copy(d, lax.rem(s + d, seqs)).wait_recv()
    own = jnp.broadcast_to(own_clip[...], (rows, rows)).astype(jnp.float32)
    own_column = own.T
    same = [
        jnp.broadcast_to(clips[s2, 0:1, :], (rows, rows)).astype(jnp.float32) == own_column
        for s2 in range(seqs)
    ]
    blocks = []
    for j in range(WINDOW):
        entry = mask_ref[c, jnp.maximum(c - j, 0)]
        seen = jnp.where((c >= j) & (entry == 1), 0.0, MASKED).astype(jnp.float32)
        for s2 in range(seqs):
            blocks.append(jnp.where(same[s2], seen, MASKED))
    bias = jnp.concatenate(blocks, axis=1)

    local[3].wait()
    relay(0)
    relay(1)
    await_others(0)

    scale = HEAD_DIM ** (-0.5)
    key_count = WINDOW * seqs * rows
    stacked = GROUP if head_count % GROUP == 0 else 1
    probabilities = []
    for h in range(0, head_count, stacked):
        if head_count % GROUP == 0:
            g = h // GROUP
            keys = kbuf[:, :, :, g * HEAD_DIM:(g + 1) * HEAD_DIM]
        else:
            at = (me * head_count + h) // GROUP - first_kv
            keys = kbuf[:, :, :, 0:HEAD_DIM]
            for g in range(1, kv_count):
                keys = jnp.where(at == g, kbuf[:, :, :, g * HEAD_DIM:(g + 1) * HEAD_DIM], keys)
        keys = keys.reshape(key_count, HEAD_DIM)
        q = jnp.concatenate(
            [qbuf[:, i * HEAD_DIM:(i + 1) * HEAD_DIM] for i in range(h, h + stacked)], axis=0
        )
        scores = lax.dot_general(
            q, keys, (((1,), (1,)), ((), ())), preferred_element_type=jnp.float32
        ) * scale
        scores = scores.reshape(stacked, rows, key_count) + bias[None]
        top = jnp.max(scores, axis=2, keepdims=True)
        p = jnp.exp(scores - top)
        total = jnp.sum(p, axis=2, keepdims=True)
        probabilities.append((
            p.astype(jnp.bfloat16).reshape(stacked * rows, key_count),
            total.reshape(stacked * rows, 1),
        ))
    await_others(1)
    for h, (p, total) in zip(range(0, head_count, stacked), probabilities):
        if head_count % GROUP == 0:
            g = h // GROUP
            values = vbuf[:, :, :, g * HEAD_DIM:(g + 1) * HEAD_DIM]
        else:
            at = (me * head_count + h) // GROUP - first_kv
            values = vbuf[:, :, :, 0:HEAD_DIM]
            for g in range(1, kv_count):
                values = jnp.where(at == g, vbuf[:, :, :, g * HEAD_DIM:(g + 1) * HEAD_DIM], values)
        values = values.reshape(key_count, HEAD_DIM)
        o = jnp.dot(p, values, preferred_element_type=jnp.float32) / total
        o = o.astype(jnp.bfloat16)
        for i in range(stacked):
            att[:, (h + i) * HEAD_DIM:(h + i + 1) * HEAD_DIM] = o[i * rows:(i + 1) * rows]

    def pass_on(way, at):
        return pltpu.make_async_remote_copy(
            src_ref=sendbuf.at[at],
            dst_ref=recvbuf.at[way, at],
            send_sem=sum_send.at[at],
            recv_sem=sum_recv.at[way, at],
            device_id={"mp": me + 1 - 2 * way},
            device_id_type=MESH,
        )

    def project(i, carry):
        to = chunk_at(i // pieces)
        at = to * pieces + lax.rem(i, pieces)
        w_copy(i).wait()
        product = jnp.dot(att[...], wbuf[i], preferred_element_type=jnp.float32)
        part[at] = product

        @pl.when((me == 0) & (to > 0))
        def _():
            sendbuf[at] = product.astype(sendbuf.dtype)
            pass_on(0, at).start()

        @pl.when((me == n - 1) & (to < n - 1))
        def _():
            sendbuf[at] = product.astype(sendbuf.dtype)
            pass_on(1, at).start()

        return carry

    lax.fori_loop(0, steps, project, 0)

    def relay_sums(i, carry):
        up = (n - 1 - i // pieces) * pieces + lax.rem(i, pieces)

        @pl.when((me > 0) & (n - 1 - i // pieces > me))
        def _():
            pass_on(0, up).wait_recv()
            sendbuf[up] = (part[up] + recvbuf[0, up].astype(jnp.float32)).astype(sendbuf.dtype)
            pass_on(0, up).start()

        @pl.when((me < n - 1) & (i // pieces < me))
        def _():
            pass_on(1, i).wait_recv()
            sendbuf[i] = (part[i] + recvbuf[1, i].astype(jnp.float32)).astype(sendbuf.dtype)
            pass_on(1, i).start()

        return carry

    lax.fori_loop(0, (n - 2) * pieces, relay_sums, 0)

    def out_copy(i):
        return pltpu.make_async_copy(
            outbuf.at[i], out_ref.at[0, :, pl.ds(i * width, width)], out_sem.at[i]
        )

    for i in range(pieces):
        at = me * pieces + i

        @pl.when(me > 0)
        def _():
            pass_on(0, at).wait_recv()
            part[at] += recvbuf[0, at].astype(jnp.float32)

        @pl.when(me < n - 1)
        def _():
            pass_on(1, at).wait_recv()
            part[at] += recvbuf[1, at].astype(jnp.float32)

        outbuf[i] = part[at].astype(outbuf.dtype)
        out_copy(i).start()

    for a in range(2):
        for j in range(1, WINDOW):
            @pl.when(c + j < spans)
            def _():
                to_span(j, a).wait_send()
            @pl.when(c >= j)
            def _():
                for d in range(1, seqs):
                    to_seq(j, d, a).wait_send()
        for d in range(1, seqs):
            to_seq(0, d, a).wait_send()
    for d in range(1, seqs):
        clip_copy(d, s).wait_send()

    def sent(i, carry):
        @pl.when(i // pieces != me)
        def _():
            pass_on(0, i).wait_send()

        return carry

    lax.fori_loop(0, steps, sent, 0)
    for i in range(pieces):
        out_copy(i).wait()


def on_device(queries, keys, values, clip_ids, block_mask, out_weight):
    spans = lax.axis_size("span")
    seqs = lax.axis_size("seq")
    n = lax.axis_size("mp")
    _, rows, local_width = queries.shape
    head_count = local_width // HEAD_DIM
    kv_total = keys.shape[2] // HEAD_DIM
    firsts = [m * head_count // GROUP for m in range(n)]
    lasts = [((m + 1) * head_count - 1) // GROUP for m in range(n)]
    kv_count = max(b - a + 1 for a, b in zip(firsts, lasts))
    kv_width = kv_count * HEAD_DIM
    depth, out_width = out_weight.shape
    chunk = out_width // n
    width = 512 if chunk % 512 == 0 else HEAD_DIM
    pieces = chunk // width
    bf16 = jnp.bfloat16
    hbm = pl.BlockSpec(memory_space=pl.ANY)
    return pl.pallas_call(
        functools.partial(kernel, spans, seqs, n, pieces, kv_count, kv_total),
        out_shape=jax.ShapeDtypeStruct((1, rows, chunk), bf16),
        in_specs=[hbm, hbm, hbm, hbm, pl.BlockSpec(memory_space=pltpu.SMEM), hbm],
        out_specs=hbm,
        scratch_shapes=[
            pltpu.VMEM((rows, local_width), bf16),
            pltpu.VMEM((WINDOW, seqs, rows, kv_width), bf16),
            pltpu.VMEM((WINDOW, seqs, rows, kv_width), bf16),
            pltpu.VMEM((1, rows), jnp.int32),
            pltpu.VMEM((seqs, 8, rows), jnp.int32),
            pltpu.VMEM((n * pieces, depth, width), bf16),
            pltpu.VMEM((rows, local_width), bf16),
            pltpu.VMEM((n * pieces, rows, width), jnp.float32),
            pltpu.VMEM((n * pieces, rows, width), bf16),
            pltpu.VMEM((2, n * pieces, rows, width), bf16),
            pltpu.VMEM((pieces, rows, width), bf16),
            pltpu.SemaphoreType.DMA((4,)),
            pltpu.SemaphoreType.DMA((n * pieces,)),
            pltpu.SemaphoreType.DMA((WINDOW, 2)),
            pltpu.SemaphoreType.DMA((WINDOW, seqs, 2)),
            pltpu.SemaphoreType.DMA((WINDOW, seqs, 2)),
            pltpu.SemaphoreType.DMA((seqs,)),
            pltpu.SemaphoreType.DMA((seqs,)),
            pltpu.SemaphoreType.DMA((n * pieces,)),
            pltpu.SemaphoreType.DMA((2, n * pieces)),
            pltpu.SemaphoreType.DMA((pieces,)),
        ],
        compiler_params=pltpu.CompilerParams(
            collective_id=0, has_side_effects=True, vmem_limit_bytes=48 * 1024 * 1024
        ),
    )(queries, keys, values, clip_ids.reshape(1, rows), block_mask, out_weight)


def solution(mesh):
    in_specs = (
        P("span", "seq", "mp"),
        P("span", "seq", None),
        P("span", "seq", None),
        P("seq"),
        P(),
        P("mp", None),
    )
    out_specs = P("span", "seq", "mp")
    return jax.shard_map(
        on_device, mesh=mesh, in_specs=in_specs, out_specs=out_specs, check_vma=False
    )
```

time: 90.3 us -> 42.9 us (0.48)
  the two profiles are of different devices: /device:TPU:0 before, /device:TPU:20 now
where the time goes in v1:
time: 42.9 us; the launch traced here: 42.7 us
  Pallas kernels  37.9 us (88%)
  local copies, waits for them, and re-layouts  4.75 us (11%)
    pallas_call x1, Pallas kernels, on_device(): pl.pallas_call(functools.partial(kernel, spans, seqs, n, pieces, kv_count...  37.9 us
    unnamed x11, local copies, waits for them, and re-layouts  4.75 us

profile of v1, /device:TPU:20, one launch (start us, length us, event | category | flops | bytes accessed | tf_op | source)
XLA Modules:
  0.0 42.7 jit_solution(2781561424681899184)
XLA Ops:
  0.0 0.0 copy-start
  0.0 0.9 %copy-done = bf16[1,64,1536]{2,1,0:T(8,128)(2,1)S(1)} copy-done((bf16[1,64,1536]{2,1,0:T(8,128)(2,1)S(1)}, bf16[1,64,1536]{2,1,0:T(8,128)(2,1)}, u32[]{:S(2)}) %copy-start) | copy-done | bytes 196632
  0.9 0.0 copy-start.1
  0.9 0.9 %copy-done.1 = bf16[1,64,1024]{2,1,0:T(8,128)(2,1)S(1)} copy-done((bf16[1,64,1024]{2,1,0:T(8,128)(2,1)S(1)}, bf16[1,64,1024]{2,1,0:T(8,128)(2,1)}, u32[]{:S(2)}) %copy-start.1) | copy-done | bytes 131096
  1.8 0.0 copy-start.2
  1.8 0.9 %copy-done.2 = bf16[1,64,1024]{2,1,0:T(8,128)(2,1)S(1)} copy-done((bf16[1,64,1024]{2,1,0:T(8,128)(2,1)S(1)}, bf16[1,64,1024]{2,1,0:T(8,128)(2,1)}, u32[]{:S(2)}) %copy-start.2) | copy-done | bytes 131096
  2.7 0.0 copy-start.3
  2.7 0.7 %copy-done.3 = s32[4,4]{1,0:T(4,128)S(1)} copy-done((s32[4,4]{1,0:T(4,128)S(1)}, s32[4,4]{1,0:T(4,128)}, u32[]{:S(2)}) %copy-start.3) | copy-done | bytes 88
  3.4 0.0 copy-start.4
  3.4 0.7 %copy-done.4 = s32[64]{0:T(128)S(1)} copy-done((s32[64]{0:T(128)S(1)}, s32[64]{0:T(128)}, u32[]{:S(2)}) %copy-start.4) | copy-done | bytes 280
  4.1 37.9 %shard_map.64 = bf16[1,64,1536]{2,1,0:T(8,128)(2,1)S(1)} custom-call(bf16[1,64,1536]{2,1,0:T(8,128)(2,1)S(1)} %copy-done, bf16[1,64,1024]{2,1,0:T(8,128)(2,1)S(1)} %copy-done.1, bf16[1,64,1024]{2,1,0:T(8,128)(2,1)S(1)} %copy-done.2, s32[1,64]{1,0:T(1,128)S(1)} %bitcast.1, s32[4,4]{1,0:T(4,128)S(1)} %copy-done.3, bf16[1536,6144]{1,0:T(8,128)(2,1)} %w_ref.1), custom_call_target="tpu_custom_call" | custom-call | tf_op jit(solution)/shard_map/pallas_call | solution.py:342
  42.0 0.7 %copy.8 = bf16[1,64,1536]{2,1,0:T(8,128)(2,1)} copy(bf16[1,64,1536]{2,1,0:T(8,128)(2,1)S(1)} %shard_map.64) | data formatting | bytes 393216
Async XLA Ops:
  0.0 0.9 %copy-start = (bf16[1,64,1536]{2,1,0:T(8,128)(2,1)S(1)}, bf16[1,64,1536]{2,1,0:T(8,128)(2,1)}, u32[]{:S(2)}) copy-start(bf16[1,64,1536]{2,1,0:T(8,128)(2,1)} %q_ref.1) | copy-start | bytes 589828
  0.9 0.9 %copy-start.1 = (bf16[1,64,1024]{2,1,0:T(8,128)(2,1)S(1)}, bf16[1,64,1024]{2,1,0:T(8,128)(2,1)}, u32[]{:S(2)}) copy-start(bf16[1,64,1024]{2,1,0:T(8,128)(2,1)} %k_ref.1) | copy-start | bytes 393220
  1.8 0.9 %copy-start.2 = (bf16[1,64,1024]{2,1,0:T(8,128)(2,1)S(1)}, bf16[1,64,1024]{2,1,0:T(8,128)(2,1)}, u32[]{:S(2)}) copy-start(bf16[1,64,1024]{2,1,0:T(8,128)(2,1)} %v_ref.1) | copy-start | bytes 393220
  2.7 0.7 %copy-start.3 = (s32[4,4]{1,0:T(4,128)S(1)}, s32[4,4]{1,0:T(4,128)}, u32[]{:S(2)}) copy-start(s32[4,4]{1,0:T(4,128)} %mask_ref.1) | copy-start | bytes 196
  3.4 0.7 %copy-start.4 = (s32[64]{0:T(128)S(1)}, s32[64]{0:T(128)}, u32[]{:S(2)}) copy-start(s32[64]{0:T(128)} %param.9) | copy-start | bytes 772

commit v2 on v1

--- a/solution.py
+++ b/solution.py
@@ -256,20 +256,26 @@
 
     lax.fori_loop(0, steps, project, 0)
 
+    lag = min(pieces, 3)
+
     def relay_sums(i, carry):
-        up = (n - 1 - i // pieces) * pieces + lax.rem(i, pieces)
-
-        @pl.when((me > 0) & (n - 1 - i // pieces > me))
+        k = jnp.maximum(i - lag * (me - 1), 0)
+        up_chunk = n - 1 - k // pieces
+        up = up_chunk * pieces + lax.rem(k, pieces)
+
+        @pl.when((me > 0) & (i >= lag * (me - 1)) & (up_chunk > me))
         def _():
             pass_on(0, up).wait_recv()
             sendbuf[up] = (part[up] + recvbuf[0, up].astype(jnp.float32)).astype(sendbuf.dtype)
             pass_on(0, up).start()
 
-        @pl.when((me < n - 1) & (i // pieces < me))
-        def _():
-            pass_on(1, i).wait_recv()
-            sendbuf[i] = (part[i] + recvbuf[1, i].astype(jnp.float32)).astype(sendbuf.dtype)
-            pass_on(1, i).start()
+        down = jnp.maximum(i - lag * (n - 2 - me), 0)
+
+        @pl.when((me < n - 1) & (i >= lag * (n - 2 - me)) & (down // pieces < me))
+        def _():
+            pass_on(1, down).wait_recv()
+            sendbuf[down] = (part[down] + recvbuf[1, down].astype(jnp.float32)).astype(sendbuf.dtype)
+            pass_on(1, down).start()
 
         return carry
 
@@ -335,7 +341,7 @@
     kv_width = kv_count * HEAD_DIM
     depth, out_width = out_weight.shape
     chunk = out_width // n
-    width = 512 if chunk % 512 == 0 else HEAD_DIM
+    width = 256 if chunk % 256 == 0 else HEAD_DIM
     pieces = chunk // width
     bf16 = jnp.bfloat16
     hbm = pl.BlockSpec(memory_space=pl.ANY)
@@ -368,7 +374,7 @@
             pltpu.SemaphoreType.DMA((pieces,)),
         ],
         compiler_params=pltpu.CompilerParams(
-            collective_id=0, has_side_effects=True, vmem_limit_bytes=48 * 1024 * 1024
+            collective_id=0, has_side_effects=True, vmem_limit_bytes=64 * 1024 * 1024
         ),
     )(queries, keys, values, clip_ids.reshape(1, rows), block_mask, out_weight)
 

time: 42.9 us -> 29.8 us (0.69)
  the two profiles are of different devices: /device:TPU:20 before, /device:TPU:12 now
where the time goes in v2:
time: 29.8 us; the launch traced here: 29.7 us
  Pallas kernels  28.1 us (94%)
  local copies, waits for them, and re-layouts  1.62 us (5%)
    pallas_call x1, Pallas kernels, on_device(): pl.pallas_call(functools.partial(kernel, spans, seqs, n, pieces, kv_count...  28.1 us
    unnamed x1, local copies, waits for them, and re-layouts  1.62 us

profile of v2, /device:TPU:12, one launch (start us, length us, event | category | flops | bytes accessed | tf_op | source)
XLA Modules:
  0.0 29.7 jit_solution(10307719221091670651)
XLA Ops:
  0.0 28.1 %shard_map.64 = bf16[1,64,1536]{2,1,0:T(8,128)(2,1)} custom-call(bf16[1,64,1536]{2,1,0:T(8,128)(2,1)} %q_ref.1, bf16[1,64,1024]{2,1,0:T(8,128)(2,1)} %k_ref.1, bf16[1,64,1024]{2,1,0:T(8,128)(2,1)} %v_ref.1, s32[1,64]{1,0:T(1,128)} %bitcast.1, s32[4,4]{1,0:T(4,128)} %mask_ref.1, bf16[1536,6144]{1,0:T(8,128)(2,1)} %w_ref.1), custom_call_target="tpu_custom_call" | custom-call | tf_op jit(solution)/shard_map/pallas_call | solution.py:348
  28.1 1.6 %copy.8 = bf16[1,64,1536]{2,1,0:T(8,128)(2,1)} copy(bf16[1,64,1536]{2,1,0:T(8,128)(2,1)} %shard_map.64) | data formatting | bytes 393216

commit v3 on v2

--- a/solution.py
+++ b/solution.py
@@ -16,7 +16,7 @@
 def kernel(
     spans, seqs, n, pieces, kv_count, kv_total,
     q_ref, k_ref, v_ref, clip_ref, mask_ref, w_ref, out_ref,
-    qbuf, kbuf, vbuf, own_clip, clips, wbuf, att, part, sendbuf, recvbuf, outbuf,
+    qbuf, kbuf, vbuf, own_clip, mask, clips, wbuf, att, part, sendbuf, recvbuf, outbuf,
     local_sem, w_sem, span_send, seq_send, kv_recv, clip_send, clip_recv, sum_send, sum_recv, out_sem,
 ):
     rows, local_width = qbuf.shape
@@ -37,17 +37,25 @@
         pltpu.make_async_copy(v_ref.at[0, :, kv_columns], vbuf.at[0, s], local_sem.at[1]),
         pltpu.make_async_copy(clip_ref, own_clip, local_sem.at[2]),
         pltpu.make_async_copy(q_ref.at[0], qbuf, local_sem.at[3]),
+        pltpu.make_async_copy(mask_ref, mask, local_sem.at[4]),
     ]
     for copy in local:
         copy.start()
 
-    turn = 2 * (2 * me // n) - 1
-
-    def chunk_at(step):
-        return lax.rem(me + turn * (step + 1) + 2 * n, n)
+    up_count = (n - 1 - me) * pieces
+    down_count = me * pieces
+    both = jnp.minimum(up_count, down_count)
+
+    def piece_at(i):
+        k = jnp.where(i < 2 * both, i // 2, i - both)
+        goes_up = jnp.where(i < 2 * both, 1 - lax.rem(i, 2), jnp.where(up_count > down_count, 1, 0))
+        moving = jnp.where(goes_up == 1, n - 1 - k // pieces, k // pieces)
+        to = jnp.where(i < up_count + down_count, moving, me)
+        return to, lax.rem(k, pieces)
 
     def w_copy(i):
-        start = chunk_at(i // pieces) * chunk + lax.rem(i, pieces) * width
+        to, piece = piece_at(i)
+        start = to * chunk + piece * width
         return pltpu.make_async_copy(
             w_ref.at[:, pl.ds(pl.multiple_of(start, HEAD_DIM), width)], wbuf.at[i], w_sem.at[i]
         )
@@ -168,9 +176,10 @@
         jnp.broadcast_to(clips[s2, 0:1, :], (rows, rows)).astype(jnp.float32) == own_column
         for s2 in range(seqs)
     ]
+    local[4].wait()
     blocks = []
     for j in range(WINDOW):
-        entry = mask_ref[c, jnp.maximum(c - j, 0)]
+        entry = mask[c, jnp.maximum(c - j, 0)]
         seen = jnp.where((c >= j) & (entry == 1), 0.0, MASKED).astype(jnp.float32)
         for s2 in range(seqs):
             blocks.append(jnp.where(same[s2], seen, MASKED))
@@ -235,9 +244,9 @@
             device_id_type=MESH,
         )
 
-    def project(i, carry):
-        to = chunk_at(i // pieces)
-        at = to * pieces + lax.rem(i, pieces)
+    def project(i):
+        to, piece = piece_at(i)
+        at = to * pieces + piece
         w_copy(i).wait()
         product = jnp.dot(att[...], wbuf[i], preferred_element_type=jnp.float32)
         part[at] = product
@@ -252,34 +261,41 @@
             sendbuf[at] = product.astype(sendbuf.dtype)
             pass_on(1, at).start()
 
-        return carry
-
-    lax.fori_loop(0, steps, project, 0)
-
-    lag = min(pieces, 3)
-
-    def relay_sums(i, carry):
-        k = jnp.maximum(i - lag * (me - 1), 0)
-        up_chunk = n - 1 - k // pieces
-        up = up_chunk * pieces + lax.rem(k, pieces)
-
-        @pl.when((me > 0) & (i >= lag * (me - 1)) & (up_chunk > me))
+    up_lag = 2 * me - 1
+    down_lag = 2 * (n - 1 - me) - 1
+
+    def relay_sums(m):
+        up = (n - 1) * pieces - jnp.maximum(m - up_lag, 0) // pieces * pieces + lax.rem(
+            jnp.maximum(m - up_lag, 0), pieces
+        )
+
+        @pl.when((me > 0) & (m >= up_lag) & (m - up_lag < up_count))
         def _():
             pass_on(0, up).wait_recv()
             sendbuf[up] = (part[up] + recvbuf[0, up].astype(jnp.float32)).astype(sendbuf.dtype)
             pass_on(0, up).start()
 
-        down = jnp.maximum(i - lag * (n - 2 - me), 0)
-
-        @pl.when((me < n - 1) & (i >= lag * (n - 2 - me)) & (down // pieces < me))
+        down = jnp.maximum(m - down_lag, 0)
+
+        @pl.when((me < n - 1) & (m >= down_lag) & (m - down_lag < down_count))
         def _():
             pass_on(1, down).wait_recv()
             sendbuf[down] = (part[down] + recvbuf[1, down].astype(jnp.float32)).astype(sendbuf.dtype)
             pass_on(1, down).start()
 
+    def project_and_relay(m, carry):
+        project(2 * m)
+        project(2 * m + 1)
+        relay_sums(m)
         return carry
 
-    lax.fori_loop(0, (n - 2) * pieces, relay_sums, 0)
+    def relay_only(m, carry):
+        relay_sums(m)
+        return carry
+
+    lax.fori_loop(0, steps // 2, project_and_relay, 0)
+    last = max((n - 1 - z) * pieces + 2 * z - 1 for z in range(1, n))
+    lax.fori_loop(steps // 2, last, relay_only, 0)
 
     def out_copy(i):
         return pltpu.make_async_copy(
@@ -348,13 +364,14 @@
     return pl.pallas_call(
         functools.partial(kernel, spans, seqs, n, pieces, kv_count, kv_total),
         out_shape=jax.ShapeDtypeStruct((1, rows, chunk), bf16),
-        in_specs=[hbm, hbm, hbm, hbm, pl.BlockSpec(memory_space=pltpu.SMEM), hbm],
+        in_specs=[hbm] * 6,
         out_specs=hbm,
         scratch_shapes=[
             pltpu.VMEM((rows, local_width), bf16),
             pltpu.VMEM((WINDOW, seqs, rows, kv_width), bf16),
             pltpu.VMEM((WINDOW, seqs, rows, kv_width), bf16),
             pltpu.VMEM((1, rows), jnp.int32),
+            pltpu.SMEM(block_mask.shape, jnp.int32),
             pltpu.VMEM((seqs, 8, rows), jnp.int32),
             pltpu.VMEM((n * pieces, depth, width), bf16),
             pltpu.VMEM((rows, local_width), bf16),
@@ -362,7 +379,7 @@
             pltpu.VMEM((n * pieces, rows, width), bf16),
             pltpu.VMEM((2, n * pieces, rows, width), bf16),
             pltpu.VMEM((pieces, rows, width), bf16),
-            pltpu.SemaphoreType.DMA((4,)),
+            pltpu.SemaphoreType.DMA((5,)),
             pltpu.SemaphoreType.DMA((n * pieces,)),
             pltpu.SemaphoreType.DMA((WINDOW, 2)),
             pltpu.SemaphoreType.DMA((WINDOW, seqs, 2)),

time: 29.8 us -> 29.5 us (0.990)
  the two profiles are of different devices: /device:TPU:12 before, /device:TPU:20 now
where the time goes in v3:
time: 29.5 us; the launch traced here: 29.4 us
  Pallas kernels  27.8 us (94%)
  local copies, waits for them, and re-layouts  1.62 us (5%)
    pallas_call x1, Pallas kernels, on_device(): pl.pallas_call(functools.partial(kernel, spans, seqs, n, pieces, kv_count...  27.8 us
    unnamed x1, local copies, waits for them, and re-layouts  1.62 us

profile of v3, /device:TPU:20, one launch (start us, length us, event | category | flops | bytes accessed | tf_op | source)
XLA Modules:
  0.0 29.4 jit_solution(4277294596469688765)
XLA Ops:
  0.0 27.8 %shard_map.64 = bf16[1,64,1536]{2,1,0:T(8,128)(2,1)} custom-call(bf16[1,64,1536]{2,1,0:T(8,128)(2,1)} %q_ref.1, bf16[1,64,1024]{2,1,0:T(8,128)(2,1)} %k_ref.1, bf16[1,64,1024]{2,1,0:T(8,128)(2,1)} %v_ref.1, s32[1,64]{1,0:T(1,128)} %bitcast.1, s32[4,4]{1,0:T(4,128)} %mask_ref.1, bf16[1536,6144]{1,0:T(8,128)(2,1)} %w_ref.1), custom_call_target="tpu_custom_call" | custom-call | tf_op jit(solution)/shard_map/pallas_call | solution.py:364
  27.8 1.6 %copy.8 = bf16[1,64,1536]{2,1,0:T(8,128)(2,1)} copy(bf16[1,64,1536]{2,1,0:T(8,128)(2,1)} %shard_map.64) | data formatting | bytes 393216

commit v4 on v3

--- a/solution.py
+++ b/solution.py
@@ -82,7 +82,8 @@
         w_copy(i).start()
         return carry
 
-    lax.fori_loop(0, steps, start_w, 0)
+    early = min(steps, 8)
+    lax.fori_loop(0, early, start_w, 0)
 
     for j in range(1, WINDOW):
         @pl.when(c < j)
@@ -219,6 +220,7 @@
             total.reshape(stacked * rows, 1),
         ))
     await_others(1)
+    lax.fori_loop(early, steps, start_w, 0)
     for h, (p, total) in zip(range(0, head_count, stacked), probabilities):
         if head_count % GROUP == 0:
             g = h // GROUP

time: 29.5 us -> 29.9 us (1.014)
  Pallas kernels: 27.8 us -> 28.1 us
    pallas_call x1, Pallas kernels: 27.8 us -> 28.1 us  [on_device(): pl.pallas_call(functools.partial(kernel, spans, seqs, n, pieces, kv_count...]
where the time goes in v4:
time: 29.9 us; the launch traced here: 29.8 us
  Pallas kernels  28.1 us (94%)
  local copies, waits for them, and re-layouts  1.62 us (5%)
    pallas_call x1, Pallas kernels, on_device(): pl.pallas_call(functools.partial(kernel, spans, seqs, n, pieces, kv_count...  28.1 us
    unnamed x1, local copies, waits for them, and re-layouts  1.62 us

profile of v4, /device:TPU:20, one launch (start us, length us, event | category | flops | bytes accessed | tf_op | source)
XLA Modules:
  0.0 29.8 jit_solution(15644368300070803413)
XLA Ops:
  0.0 28.1 %shard_map.64 = bf16[1,64,1536]{2,1,0:T(8,128)(2,1)} custom-call(bf16[1,64,1536]{2,1,0:T(8,128)(2,1)} %q_ref.1, bf16[1,64,1024]{2,1,0:T(8,128)(2,1)} %k_ref.1, bf16[1,64,1024]{2,1,0:T(8,128)(2,1)} %v_ref.1, s32[1,64]{1,0:T(1,128)} %bitcast.1, s32[4,4]{1,0:T(4,128)} %mask_ref.1, bf16[1536,6144]{1,0:T(8,128)(2,1)} %w_ref.1), custom_call_target="tpu_custom_call" | custom-call | tf_op jit(solution)/shard_map/pallas_call | solution.py:366
  28.1 1.6 %copy.8 = bf16[1,64,1536]{2,1,0:T(8,128)(2,1)} copy(bf16[1,64,1536]{2,1,0:T(8,128)(2,1)} %shard_map.64) | data formatting | bytes 393216

commit v5 on v3

--- a/solution.py
+++ b/solution.py
@@ -18,16 +18,19 @@
     q_ref, k_ref, v_ref, clip_ref, mask_ref, w_ref, out_ref,
     qbuf, kbuf, vbuf, own_clip, mask, clips, wbuf, att, part, sendbuf, recvbuf, outbuf,
     local_sem, w_sem, span_send, seq_send, kv_recv, clip_send, clip_recv, sum_send, sum_recv, out_sem,
+    att_send, att_recv, out_send, out_recv,
 ):
     rows, local_width = qbuf.shape
     head_count = local_width // HEAD_DIM
     width = wbuf.shape[2]
-    chunk = width * pieces
+    half = width * pieces
     kv_width = kv_count * HEAD_DIM
     steps = n * pieces
     c = lax.axis_index("span")
     s = lax.axis_index("seq")
     me = lax.axis_index("mp")
+    core = lax.rem(s, 2)
+    sibling = {"seq": s + 1 - 2 * core}
 
     first_kv = jnp.minimum(me * head_count // GROUP, kv_total - kv_count)
     kv_columns = pl.ds(pl.multiple_of(first_kv * HEAD_DIM, HEAD_DIM), kv_width)
@@ -55,7 +58,7 @@
 
     def w_copy(i):
         to, piece = piece_at(i)
-        start = to * chunk + piece * width
+        start = (to * 2 + core) * half + piece * width
         return pltpu.make_async_copy(
             w_ref.at[:, pl.ds(pl.multiple_of(start, HEAD_DIM), width)], wbuf.at[i], w_sem.at[i]
         )
@@ -218,6 +221,20 @@
             p.astype(jnp.bfloat16).reshape(stacked * rows, key_count),
             total.reshape(stacked * rows, 1),
         ))
+    att_heads = GROUP if head_count % GROUP == 0 else head_count
+    att_parts = head_count // att_heads
+
+    def att_copy(i, source):
+        columns = pl.ds(i * att_heads * HEAD_DIM, att_heads * HEAD_DIM)
+        return pltpu.make_async_remote_copy(
+            src_ref=att.at[source, :, columns],
+            dst_ref=att.at[source, :, columns],
+            send_sem=att_send.at[i],
+            recv_sem=att_recv.at[i],
+            device_id=sibling,
+            device_id_type=MESH,
+        )
+
     await_others(1)
     for h, (p, total) in zip(range(0, head_count, stacked), probabilities):
         if head_count % GROUP == 0:
@@ -232,7 +249,11 @@
         o = jnp.dot(p, values, preferred_element_type=jnp.float32) / total
         o = o.astype(jnp.bfloat16)
         for i in range(stacked):
-            att[:, (h + i) * HEAD_DIM:(h + i + 1) * HEAD_DIM] = o[i * rows:(i + 1) * rows]
+            att[core, :, (h + i) * HEAD_DIM:(h + i + 1) * HEAD_DIM] = o[i * rows:(i + 1) * rows]
+        if (h + stacked) % att_heads == 0:
+            att_copy((h + stacked) // att_heads - 1, core).start()
+    for i in range(att_parts):
+        att_copy(i, 1 - core).wait_recv()
 
     def pass_on(way, at):
         return pltpu.make_async_remote_copy(
@@ -248,7 +269,9 @@
         to, piece = piece_at(i)
         at = to * pieces + piece
         w_copy(i).wait()
-        product = jnp.dot(att[...], wbuf[i], preferred_element_type=jnp.float32)
+        product = jnp.dot(
+            att[...].reshape(2 * rows, local_width), wbuf[i], preferred_element_type=jnp.float32
+        )
         part[at] = product
 
         @pl.when((me == 0) & (to > 0))
@@ -297,9 +320,24 @@
     last = max((n - 1 - z) * pieces + 2 * z - 1 for z in range(1, n))
     lax.fori_loop(steps // 2, last, relay_only, 0)
 
+    def out_columns(i, of):
+        return pl.ds(pl.multiple_of(of * half + i * width, HEAD_DIM), width)
+
     def out_copy(i):
         return pltpu.make_async_copy(
-            outbuf.at[i], out_ref.at[0, :, pl.ds(i * width, width)], out_sem.at[i]
+            outbuf.at[i, pl.ds(pl.multiple_of(core * rows, rows), rows)],
+            out_ref.at[0, :, out_columns(i, core)],
+            out_sem.at[i],
+        )
+
+    def out_to_sibling(i, of):
+        return pltpu.make_async_remote_copy(
+            src_ref=outbuf.at[i, pl.ds(pl.multiple_of((1 - core) * rows, rows), rows)],
+            dst_ref=out_ref.at[0, :, out_columns(i, of)],
+            send_sem=out_send.at[i],
+            recv_sem=out_recv.at[i],
+            device_id=sibling,
+            device_id_type=MESH,
         )
 
     for i in range(pieces):
@@ -316,6 +354,7 @@
             part[at] += recvbuf[1, at].astype(jnp.float32)
 
         outbuf[i] = part[at].astype(outbuf.dtype)
+        out_to_sibling(i, core).start()
         out_copy(i).start()
 
     for a in range(2):
@@ -340,8 +379,12 @@
         return carry
 
     lax.fori_loop(0, steps, sent, 0)
+    for i in range(att_parts):
+        att_copy(i, core).wait_send()
     for i in range(pieces):
         out_copy(i).wait()
+        out_to_sibling(i, core).wait_send()
+        out_to_sibling(i, 1 - core).wait_recv()
 
 
 def on_device(queries, keys, values, clip_ids, block_mask, out_weight):
@@ -357,8 +400,8 @@
     kv_width = kv_count * HEAD_DIM
     depth, out_width = out_weight.shape
     chunk = out_width // n
-    width = 256 if chunk % 256 == 0 else HEAD_DIM
-    pieces = chunk // width
+    width = 256 if chunk % 512 == 0 else HEAD_DIM
+    pieces = chunk // 2 // width
     bf16 = jnp.bfloat16
     hbm = pl.BlockSpec(memory_space=pl.ANY)
     return pl.pallas_call(
@@ -374,11 +417,11 @@
             pltpu.SMEM(block_mask.shape, jnp.int32),
             pltpu.VMEM((seqs, 8, rows), jnp.int32),
             pltpu.VMEM((n * pieces, depth, width), bf16),
-            pltpu.VMEM((rows, local_width), bf16),
-            pltpu.VMEM((n * pieces, rows, width), jnp.float32),
-            pltpu.VMEM((n * pieces, rows, width), bf16),
-            pltpu.VMEM((2, n * pieces, rows, width), bf16),
-            pltpu.VMEM((pieces, rows, width), bf16),
+            pltpu.VMEM((2, rows, local_width), bf16),
+            pltpu.VMEM((n * pieces, 2 * rows, width), jnp.float32),
+            pltpu.VMEM((n * pieces, 2 * rows, width), bf16),
+            pltpu.VMEM((2, n * pieces, 2 * rows, width), bf16),
+            pltpu.VMEM((pieces, 2 * rows, width), bf16),
             pltpu.SemaphoreType.DMA((5,)),
             pltpu.SemaphoreType.DMA((n * pieces,)),
             pltpu.SemaphoreType.DMA((WINDOW, 2)),
@@ -388,6 +431,10 @@
             pltpu.SemaphoreType.DMA((seqs,)),
             pltpu.SemaphoreType.DMA((n * pieces,)),
             pltpu.SemaphoreType.DMA((2, n * pieces)),
+            pltpu.SemaphoreType.DMA((pieces,)),
+            pltpu.SemaphoreType.DMA((local_width // HEAD_DIM,)),
+            pltpu.SemaphoreType.DMA((local_width // HEAD_DIM,)),
+            pltpu.SemaphoreType.DMA((pieces,)),
             pltpu.SemaphoreType.DMA((pieces,)),
         ],
         compiler_params=pltpu.CompilerParams(

time: 29.5 us -> 28.1 us (0.953)
  the two profiles are of different devices: /device:TPU:20 before, /device:TPU:13 now
where the time goes in v5:
time: 28.1 us; the launch traced here: 27.9 us
  Pallas kernels  26.3 us (94%)
  local copies, waits for them, and re-layouts  1.62 us (6%)
    pallas_call x1, Pallas kernels, on_device(): pl.pallas_call(functools.partial(kernel, spans, seqs, n, pieces, kv_count...  26.3 us
    unnamed x1, local copies, waits for them, and re-layouts  1.62 us

profile of v5, /device:TPU:13, one launch (start us, length us, event | category | flops | bytes accessed | tf_op | source)
XLA Modules:
  0.0 27.9 jit_solution(13385955344367922565)
XLA Ops:
  0.0 26.3 %shard_map.64 = bf16[1,64,1536]{2,1,0:T(8,128)(2,1)} custom-call(bf16[1,64,1536]{2,1,0:T(8,128)(2,1)} %q_ref.1, bf16[1,64,1024]{2,1,0:T(8,128)(2,1)} %k_ref.1, bf16[1,64,1024]{2,1,0:T(8,128)(2,1)} %v_ref.1, s32[1,64]{1,0:T(1,128)} %bitcast.1, s32[4,4]{1,0:T(4,128)} %mask_ref.1, bf16[1536,6144]{1,0:T(8,128)(2,1)} %w_ref.1), custom_call_target="tpu_custom_call" | custom-call | tf_op jit(solution)/shard_map/pallas_call | solution.py:407
  26.3 1.6 %copy.8 = bf16[1,64,1536]{2,1,0:T(8,128)(2,1)} copy(bf16[1,64,1536]{2,1,0:T(8,128)(2,1)} %shard_map.64) | data formatting | bytes 393216

commit v6 on v5

v6 whole, which is shorter than its diff:
```python
import functools
import math
import jax
import jax.numpy as jnp
from jax import lax
from jax.experimental import pallas as pl
from jax.experimental.pallas import tpu as pltpu
from jax.sharding import PartitionSpec as P

HEAD_DIM = 128
WINDOW = 3
GROUP = 6
MASKED = -1e30
MESH = pl.DeviceIdType.MESH


def kernel(
    spans, seqs, n, pieces,
    q_ref, k_ref, v_ref, clip_ref, mask_ref, w_ref, out_ref,
    qbuf, q_other, kbuf, vbuf, other, own_clip, mask, clips, wbuf, att, part, sendbuf, recvbuf, outbuf,
    local_sem, w_sem, q_sem, kv_send, kv_recv, clip_send, clip_recv, sum_send, sum_recv, out_sem,
    att_send, att_recv, out_send, out_recv,
):
    _, rows, local_width = q_ref.shape
    head_count = local_width // HEAD_DIM
    width = wbuf.shape[2]
    half = width * pieces
    steps = n * pieces
    c = lax.axis_index("span")
    s = lax.axis_index("seq")
    me = lax.axis_index("mp")
    core = lax.rem(s, 2)
    sibling = {"seq": s + 1 - 2 * core}

    my_heads = head_count // 2
    buddy = s + 1 - 2 * core

    def kv_columns(of):
        group = (me * head_count + of * my_heads) // GROUP
        return pl.ds(pl.multiple_of(group * HEAD_DIM, HEAD_DIM), HEAD_DIM)

    def q_columns(of):
        return pl.ds(pl.multiple_of(of * my_heads * HEAD_DIM, HEAD_DIM), my_heads * HEAD_DIM)

    local = [
        pltpu.make_async_copy(k_ref.at[0, :, kv_columns(core)], kbuf.at[0, s], local_sem.at[0]),
        pltpu.make_async_copy(k_ref.at[0, :, kv_columns(1 - core)], other.at[0], local_sem.at[1]),
        pltpu.make_async_copy(q_ref.at[0, :, q_columns(1 - core)], q_other, local_sem.at[2]),
        pltpu.make_async_copy(v_ref.at[0, :, kv_columns(core)], vbuf.at[0, s], local_sem.at[3]),
        pltpu.make_async_copy(v_ref.at[0, :, kv_columns(1 - core)], other.at[1], local_sem.at[4]),
        pltpu.make_async_copy(clip_ref, own_clip, local_sem.at[5]),
        pltpu.make_async_copy(mask_ref, mask, local_sem.at[6]),
        pltpu.make_async_copy(q_ref.at[0, :, q_columns(core)], qbuf.at[core], local_sem.at[7]),
    ]
    for copy in local:
        copy.start()

    up_count = (n - 1 - me) * pieces
    down_count = me * pieces
    both = jnp.minimum(up_count, down_count)

    def piece_at(i):
        k = jnp.where(i < 2 * both, i // 2, i - both)
        goes_up = jnp.where(i < 2 * both, 1 - lax.rem(i, 2), jnp.where(up_count > down_count, 1, 0))
        moving = jnp.where(goes_up == 1, n - 1 - k // pieces, k // pieces)
        to = jnp.where(i < up_count + down_count, moving, me)
        return to, lax.rem(k, pieces)

    def w_copy(i):
        to, piece = piece_at(i)
        start = (to * 2 + core) * half + piece * width
        return pltpu.make_async_copy(
            w_ref.at[:, pl.ds(pl.multiple_of(start, HEAD_DIM), width)], wbuf.at[i], w_sem.at[i]
        )

    barrier = pltpu.get_barrier_semaphore()
    for j in range(1, WINDOW):
        @pl.when(c >= j)
        def _():
            for s2 in range(seqs):
                pl.semaphore_signal(
                    barrier, inc=1, device_id={"span": c - j, "seq": s2}, device_id_type=MESH
                )
    for d in range(1, seqs):
        pl.semaphore_signal(
            barrier, inc=1, device_id={"seq": lax.rem(s + d, seqs)}, device_id_type=MESH
        )

    @pl.when(me > 0)
    def _():
        pl.semaphore_signal(barrier, inc=1, device_id={"mp": me - 1}, device_id_type=MESH)

    @pl.when(me < n - 1)
    def _():
        pl.semaphore_signal(barrier, inc=1, device_id={"mp": me + 1}, device_id_type=MESH)

    def start_w(i, carry):
        w_copy(i).start()
        return carry

    lax.fori_loop(0, steps, start_w, 0)

    for j in range(1, WINDOW):
        @pl.when(c < j)
        def _():
            kbuf[j] = jnp.zeros(kbuf.shape[1:], kbuf.dtype)
            vbuf[j] = jnp.zeros(vbuf.shape[1:], vbuf.dtype)

    local[5].wait()
    clips[s] = jnp.broadcast_to(own_clip[...], clips.shape[1:])
    for i in range(5):
        local[i].wait()
    later_spans = jnp.minimum(spans - 1 - c, WINDOW - 1)
    z_neighbours = jnp.minimum(me, 1) + jnp.minimum(n - 1 - me, 1)
    pl.semaphore_wait(barrier, seqs - 1 + seqs * later_spans + z_neighbours)

    bufs = (kbuf, vbuf)

    def kv_copy(j, d, a):
        source = bufs[a].at[0, s] if d % 2 == 0 else other.at[a]
        return pltpu.make_async_remote_copy(
            src_ref=source,
            dst_ref=bufs[a].at[j, s],
            send_sem=kv_send.at[j, d, a],
            recv_sem=kv_recv.at[j, s, a],
            device_id={"span": c + j, "seq": lax.rem(s + d, seqs)},
            device_id_type=MESH,
        )

    def arrival(j, s2, a):
        return pltpu.make_async_remote_copy(
            src_ref=bufs[a].at[j, s2],
            dst_ref=bufs[a].at[j, s2],
            send_sem=kv_send.at[0, 0, a],
            recv_sem=kv_recv.at[j, s2, a],
            device_id={"seq": buddy},
            device_id_type=MESH,
        )

    def clip_copy(d, source):
        return pltpu.make_async_remote_copy(
            src_ref=clips.at[source],
            dst_ref=clips.at[source],
            send_sem=clip_send.at[d],
            recv_sem=clip_recv.at[source],
            device_id={"seq": lax.rem(s + d, seqs)},
            device_id_type=MESH,
        )

    def q_copy(at):
        return pltpu.make_async_remote_copy(
            src_ref=q_other,
            dst_ref=qbuf.at[at],
            send_sem=q_sem.at[0],
            recv_sem=q_sem.at[1],
            device_id=sibling,
            device_id_type=MESH,
        )

    for a in range(2):
        for j in range(WINDOW - 1, 0, -1):
            @pl.when(c + j < spans)
            def _():
                for d in range(seqs):
                    kv_copy(j, d, a).start()
        for d in range(1, seqs):
            kv_copy(0, d, a).start()
        if a == 0:
            q_copy(core).start()
            for d in range(1, seqs):
                clip_copy(d, s).start()

    def await_block(j, a):
        if j == 0:
            for d in range(1, seqs):
                arrival(0, lax.rem(s + d, seqs), a).wait_recv()
        else:
            @pl.when(c >= j)
            def _():
                for s2 in range(seqs):
                    arrival(j, s2, a).wait_recv()

    for d in range(1, seqs):
        clip_copy(d, lax.rem(s + d, seqs)).wait_recv()
    local[6].wait()

    def clip_square(s2):
        return jnp.broadcast_to(clips[s2, 0:1, :], (rows, rows)).astype(jnp.float32)

    columns = [clip_square(s - core + r).T for r in range(2)]
    same = [[clip_square(s2) == column for s2 in range(seqs)] for column in columns]

    local[7].wait()
    q_copy(1 - core).wait_recv()
    queries = jnp.concatenate(
        [
            qbuf[:, :, i * HEAD_DIM:(i + 1) * HEAD_DIM].reshape(2 * rows, HEAD_DIM)
            for i in range(my_heads)
        ],
        axis=0,
    )
    piece = seqs * rows
    scores = []
    for j in range(WINDOW):
        entry = mask[c, jnp.maximum(c - j, 0)]
        seen = jnp.where((c >= j) & (entry == 1), 0.0, MASKED).astype(jnp.float32)
        bias = jnp.concatenate(
            [
                jnp.concatenate([jnp.where(same[r][s2], seen, MASKED) for s2 in range(seqs)], axis=1)
                for r in range(2)
            ],
            axis=0,
        )
        await_block(j, 0)
        dots = lax.dot_general(
            queries, kbuf[j].reshape(piece, HEAD_DIM), (((1,), (1,)), ((), ())),
            preferred_element_type=jnp.float32,
        )
        scores.append(dots.reshape(my_heads, 2 * rows, piece) + bias[None])
    scores = jnp.concatenate(scores, axis=2)
    top = jnp.max(scores, axis=2, keepdims=True)
    scale = HEAD_DIM ** (-0.5) * math.log2(math.e)
    weights = jnp.exp2((scores - top) * scale).astype(jnp.bfloat16)
    for j in range(WINDOW):
        await_block(j, 1)
    key_count = WINDOW * piece
    values = jnp.concatenate(
        [vbuf[...].reshape(key_count, HEAD_DIM), jnp.ones((key_count, HEAD_DIM), jnp.bfloat16)],
        axis=1,
    )

    att_parts = 2
    att_heads = my_heads // att_parts

    def att_copy(i, source):
        part_columns = pl.ds(i * att_heads * HEAD_DIM, att_heads * HEAD_DIM)
        return pltpu.make_async_remote_copy(
            src_ref=att.at[source, :, part_columns],
            dst_ref=att.at[source, :, part_columns],
            send_sem=att_send.at[i],
            recv_sem=att_recv.at[i],
            device_id=sibling,
            device_id_type=MESH,
        )

    for i in range(att_parts):
        heads = slice(i * att_heads, (i + 1) * att_heads)
        both_sums = jnp.dot(
            weights[heads].reshape(att_heads * 2 * rows, key_count), values,
            preferred_element_type=jnp.float32,
        )
        o = (both_sums[:, :HEAD_DIM] / both_sums[:, HEAD_DIM:]).astype(jnp.bfloat16)
        for h in range(att_heads):
            at = (i * att_heads + h) * HEAD_DIM
            att[core, :, at:at + HEAD_DIM] = o[h * 2 * rows:(h + 1) * 2 * rows]
        att_copy(i, core).start()
    for i in range(att_parts):
        att_copy(i, 1 - core).wait_recv()

    def pass_on(way, at):
        return pltpu.make_async_remote_copy(
            src_ref=sendbuf.at[at],
            dst_ref=recvbuf.at[way, at],
            send_sem=sum_send.at[at],
            recv_sem=sum_recv.at[way, at],
            device_id={"mp": me + 1 - 2 * way},
            device_id_type=MESH,
        )

    def project(i):
        to, piece = piece_at(i)
        at = to * pieces + piece
        w_copy(i).wait()
        product = jnp.dot(
            jnp.concatenate([att[0], att[1]], axis=1), wbuf[i], preferred_element_type=jnp.float32
        )
        part[at] = product

        @pl.when((me == 0) & (to > 0))
        def _():
            sendbuf[at] = product.astype(sendbuf.dtype)
            pass_on(0, at).start()

        @pl.when((me == n - 1) & (to < n - 1))
        def _():
            sendbuf[at] = product.astype(sendbuf.dtype)
            pass_on(1, at).start()

    up_lag = 2 * me - 1
    down_lag = 2 * (n - 1 - me) - 1

    def relay_sums(m):
        up = (n - 1) * pieces - jnp.maximum(m - up_lag, 0) // pieces * pieces + lax.rem(
            jnp.maximum(m - up_lag, 0), pieces
        )

        @pl.when((me > 0) & (m >= up_lag) & (m - up_lag < up_count))
        def _():
            pass_on(0, up).wait_recv()
            sendbuf[up] = (part[up] + recvbuf[0, up].astype(jnp.float32)).astype(sendbuf.dtype)
            pass_on(0, up).start()

        down = jnp.maximum(m - down_lag, 0)

        @pl.when((me < n - 1) & (m >= down_lag) & (m - down_lag < down_count))
        def _():
            pass_on(1, down).wait_recv()
            sendbuf[down] = (part[down] + recvbuf[1, down].astype(jnp.float32)).astype(sendbuf.dtype)
            pass_on(1, down).start()

    def project_and_relay(m, carry):
        project(2 * m)
        project(2 * m + 1)
        relay_sums(m)
        return carry

    def relay_only(m, carry):
        relay_sums(m)
        return carry

    lax.fori_loop(0, steps // 2, project_and_relay, 0)
    last = max((n - 1 - z) * pieces + 2 * z - 1 for z in range(1, n))
    lax.fori_loop(steps // 2, last, relay_only, 0)

    def out_columns(i, of):
        return pl.ds(pl.multiple_of(of * half + i * width, HEAD_DIM), width)

    def out_copy(i):
        return pltpu.make_async_copy(
            outbuf.at[i, pl.ds(pl.multiple_of(core * rows, rows), rows)],
            out_ref.at[0, :, out_columns(i, core)],
            out_sem.at[i],
        )

    def out_to_sibling(i, of):
        return pltpu.make_async_remote_copy(
            src_ref=outbuf.at[i, pl.ds(pl.multiple_of((1 - core) * rows, rows), rows)],
            dst_ref=out_ref.at[0, :, out_columns(i, of)],
            send_sem=out_send.at[i],
            recv_sem=out_recv.at[i],
            device_id=sibling,
            device_id_type=MESH,
        )

    for i in range(pieces):
        at = me * pieces + i

        @pl.when(me > 0)
        def _():
            pass_on(0, at).wait_recv()
            part[at] += recvbuf[0, at].astype(jnp.float32)

        @pl.when(me < n - 1)
        def _():
            pass_on(1, at).wait_recv()
            part[at] += recvbuf[1, at].astype(jnp.float32)

        outbuf[i] = part[at].astype(outbuf.dtype)
        out_to_sibling(i, core).start()
        out_copy(i).start()

    for a in range(2):
        for j in range(1, WINDOW):
            @pl.when(c + j < spans)
            def _():
                for d in range(seqs):
                    kv_copy(j, d, a).wait_send()
        for d in range(1, seqs):
            kv_copy(0, d, a).wait_send()
    q_copy(core).wait_send()
    for d in range(1, seqs):
        clip_copy(d, s).wait_send()

    def sent(i, carry):
        @pl.when(i // pieces != me)
        def _():
            pass_on(0, i).wait_send()

        return carry

    lax.fori_loop(0, steps, sent, 0)
    for i in range(att_parts):
        att_copy(i, core).wait_send()
    for i in range(pieces):
        out_copy(i).wait()
        out_to_sibling(i, core).wait_send()
        out_to_sibling(i, 1 - core).wait_recv()


def on_device(queries, keys, values, clip_ids, block_mask, out_weight):
    spans = lax.axis_size("span")
    seqs = lax.axis_size("seq")
    n = lax.axis_size("mp")
    _, rows, local_width = queries.shape
    assert GROUP % (local_width // HEAD_DIM // 2) == 0
    depth, out_width = out_weight.shape
    chunk = out_width // n
    width = 256 if chunk % 512 == 0 else HEAD_DIM
    pieces = chunk // 2 // width
    bf16 = jnp.bfloat16
    hbm = pl.BlockSpec(memory_space=pl.ANY)
    return pl.pallas_call(
        functools.partial(kernel, spans, seqs, n, pieces),
        out_shape=jax.ShapeDtypeStruct((1, rows, chunk), bf16),
        in_specs=[hbm] * 6,
        out_specs=hbm,
        scratch_shapes=[
            pltpu.VMEM((2, rows, local_width // 2), bf16),
            pltpu.VMEM((rows, local_width // 2), bf16),
            pltpu.VMEM((WINDOW, seqs, rows, HEAD_DIM), bf16),
            pltpu.VMEM((WINDOW, seqs, rows, HEAD_DIM), bf16),
            pltpu.VMEM((2, rows, HEAD_DIM), bf16),
            pltpu.VMEM((1, rows), jnp.int32),
            pltpu.SMEM(block_mask.shape, jnp.int32),
            pltpu.VMEM((seqs, 8, rows), jnp.int32),
            pltpu.VMEM((n * pieces, depth, width), bf16),
            pltpu.VMEM((2, 2 * rows, local_width // 2), bf16),
            pltpu.VMEM((n * pieces, 2 * rows, width), jnp.float32),
            pltpu.VMEM((n * pieces, 2 * rows, width), bf16),
            pltpu.VMEM((2, n * pieces, 2 * rows, width), bf16),
            pltpu.VMEM((pieces, 2 * rows, width), bf16),
            pltpu.SemaphoreType.DMA((8,)),
            pltpu.SemaphoreType.DMA((n * pieces,)),
            pltpu.SemaphoreType.DMA((2,)),
            pltpu.SemaphoreType.DMA((WINDOW, seqs, 2)),
            pltpu.SemaphoreType.DMA((WINDOW, seqs, 2)),
            pltpu.SemaphoreType.DMA((seqs,)),
            pltpu.SemaphoreType.DMA((seqs,)),
            pltpu.SemaphoreType.DMA((n * pieces,)),
            pltpu.SemaphoreType.DMA((2, n * pieces)),
            pltpu.SemaphoreType.DMA((pieces,)),
            pltpu.SemaphoreType.DMA((2,)),
            pltpu.SemaphoreType.DMA((2,)),
            pltpu.SemaphoreType.DMA((pieces,)),
            pltpu.SemaphoreType.DMA((pieces,)),
        ],
        compiler_params=pltpu.CompilerParams(
            collective_id=0, has_side_effects=True, vmem_limit_bytes=64 * 1024 * 1024
        ),
    )(queries, keys, values, clip_ids.reshape(1, rows), block_mask, out_weight)


def solution(mesh):
    in_specs = (
        P("span", "seq", "mp"),
        P("span", "seq", None),
        P("span", "seq", None),
        P("seq"),
        P(),
        P("mp", None),
    )
    out_specs = P("span", "seq", "mp")
    return jax.shard_map(
        on_device, mesh=mesh, in_specs=in_specs, out_specs=out_specs, check_vma=False
    )
```

time: 28.1 us -> 27.1 us (0.964)
  the two profiles are of different devices: /device:TPU:13 before, /device:TPU:21 now
where the time goes in v6:
time: 27.1 us; the launch traced here: 26.9 us
  Pallas kernels  25.3 us (93%)
  local copies, waits for them, and re-layouts  1.62 us (6%)
    pallas_call x1, Pallas kernels, on_device(): pl.pallas_call(functools.partial(kernel, spans, seqs, n, pieces), out_sha...  25.3 us
    unnamed x1, local copies, waits for them, and re-layouts  1.62 us

profile of v6, /device:TPU:21, one launch (start us, length us, event | category | flops | bytes accessed | tf_op | source)
XLA Modules:
  0.0 26.9 jit_solution(12926806066404367325)
XLA Ops:
  0.0 25.3 %shard_map.64 = bf16[1,64,1536]{2,1,0:T(8,128)(2,1)} custom-call(bf16[1,64,1536]{2,1,0:T(8,128)(2,1)} %q_ref.1, bf16[1,64,1024]{2,1,0:T(8,128)(2,1)} %k_ref.1, bf16[1,64,1024]{2,1,0:T(8,128)(2,1)} %v_ref.1, s32[1,64]{1,0:T(1,128)} %bitcast.1, s32[4,4]{1,0:T(4,128)} %mask_ref.1, bf16[1536,6144]{1,0:T(8,128)(2,1)} %w_ref.1), custom_call_target="tpu_custom_call" | custom-call | tf_op jit(solution)/shard_map/pallas_call | solution.py:402
  25.3 1.6 %copy.8 = bf16[1,64,1536]{2,1,0:T(8,128)(2,1)} copy(bf16[1,64,1536]{2,1,0:T(8,128)(2,1)} %shard_map.64) | data formatting | bytes 393216

commit v7 on v6

--- a/solution.py
+++ b/solution.py
@@ -32,6 +32,27 @@
     core = lax.rem(s, 2)
     sibling = {"seq": s + 1 - 2 * core}
 
+    barrier = pltpu.get_barrier_semaphore()
+    for j in range(1, WINDOW):
+        @pl.when(c >= j)
+        def _():
+            for s2 in range(seqs):
+                pl.semaphore_signal(
+                    barrier, inc=1, device_id={"span": c - j, "seq": s2}, device_id_type=MESH
+                )
+    for d in range(1, seqs):
+        pl.semaphore_signal(
+            barrier, inc=1, device_id={"seq": lax.rem(s + d, seqs)}, device_id_type=MESH
+        )
+
+    @pl.when(me > 0)
+    def _():
+        pl.semaphore_signal(barrier, inc=1, device_id={"mp": me - 1}, device_id_type=MESH)
+
+    @pl.when(me < n - 1)
+    def _():
+        pl.semaphore_signal(barrier, inc=1, device_id={"mp": me + 1}, device_id_type=MESH)
+
     my_heads = head_count // 2
     buddy = s + 1 - 2 * core
 
@@ -73,33 +94,6 @@
             w_ref.at[:, pl.ds(pl.multiple_of(start, HEAD_DIM), width)], wbuf.at[i], w_sem.at[i]
         )
 
-    barrier = pltpu.get_barrier_semaphore()
-    for j in range(1, WINDOW):
-        @pl.when(c >= j)
-        def _():
-            for s2 in range(seqs):
-                pl.semaphore_signal(
-                    barrier, inc=1, device_id={"span": c - j, "seq": s2}, device_id_type=MESH
-                )
-    for d in range(1, seqs):
-        pl.semaphore_signal(
-            barrier, inc=1, device_id={"seq": lax.rem(s + d, seqs)}, device_id_type=MESH
-        )
-
-    @pl.when(me > 0)
-    def _():
-        pl.semaphore_signal(barrier, inc=1, device_id={"mp": me - 1}, device_id_type=MESH)
-
-    @pl.when(me < n - 1)
-    def _():
-        pl.semaphore_signal(barrier, inc=1, device_id={"mp": me + 1}, device_id_type=MESH)
-
-    def start_w(i, carry):
-        w_copy(i).start()
-        return carry
-
-    lax.fori_loop(0, steps, start_w, 0)
-
     for j in range(1, WINDOW):
         @pl.when(c < j)
         def _():
@@ -108,7 +102,7 @@
 
     local[5].wait()
     clips[s] = jnp.broadcast_to(own_clip[...], clips.shape[1:])
-    for i in range(5):
+    for i in range(2):
         local[i].wait()
     later_spans = jnp.minimum(spans - 1 - c, WINDOW - 1)
     z_neighbours = jnp.minimum(me, 1) + jnp.minimum(n - 1 - me, 1)
@@ -158,7 +152,7 @@
         )
 
     for a in range(2):
-        for j in range(WINDOW - 1, 0, -1):
+        for j in range(1, WINDOW):
             @pl.when(c + j < spans)
             def _():
                 for d in range(seqs):
@@ -166,9 +160,18 @@
         for d in range(1, seqs):
             kv_copy(0, d, a).start()
         if a == 0:
+            local[2].wait()
             q_copy(core).start()
             for d in range(1, seqs):
                 clip_copy(d, s).start()
+            local[3].wait()
+            local[4].wait()
+
+    def start_w(i, carry):
+        w_copy(i).start()
+        return carry
+
+    lax.fori_loop(0, steps, start_w, 0)
 
     def await_block(j, a):
         if j == 0:
@@ -355,7 +358,7 @@
             pass_on(1, at).wait_recv()
             part[at] += recvbuf[1, at].astype(jnp.float32)
 
-        outbuf[i] = part[at].astype(outbuf.dtype)
+        outbuf[i] = part[at]
         out_to_sibling(i, core).start()
         out_copy(i).start()
 
@@ -399,9 +402,9 @@
     pieces = chunk // 2 // width
     bf16 = jnp.bfloat16
     hbm = pl.BlockSpec(memory_space=pl.ANY)
-    return pl.pallas_call(
+    total = pl.pallas_call(
         functools.partial(kernel, spans, seqs, n, pieces),
-        out_shape=jax.ShapeDtypeStruct((1, rows, chunk), bf16),
+        out_shape=jax.ShapeDtypeStruct((1, rows, chunk), jnp.float32),
         in_specs=[hbm] * 6,
         out_specs=hbm,
         scratch_shapes=[
@@ -418,7 +421,7 @@
             pltpu.VMEM((n * pieces, 2 * rows, width), jnp.float32),
             pltpu.VMEM((n * pieces, 2 * rows, width), bf16),
             pltpu.VMEM((2, n * pieces, 2 * rows, width), bf16),
-            pltpu.VMEM((pieces, 2 * rows, width), bf16),
+            pltpu.VMEM((pieces, 2 * rows, width), jnp.float32),
             pltpu.SemaphoreType.DMA((8,)),
             pltpu.SemaphoreType.DMA((n * pieces,)),
             pltpu.SemaphoreType.DMA((2,)),
@@ -438,6 +441,7 @@
             collective_id=0, has_side_effects=True, vmem_limit_bytes=64 * 1024 * 1024
         ),
     )(queries, keys, values, clip_ids.reshape(1, rows), block_mask, out_weight)
+    return total.astype(bf16)
 
 
 def solution(mesh):

time: 27.1 us -> 27.2 us (level)
  other arithmetic: 0 us -> 1.69 us
  local copies, waits for them, and re-layouts: 1.62 us -> 0 us
    convert_element_type x0 -> x1, other arithmetic: none -> 1.69 us  [on_device(): return total.astype(bf16)]
    unnamed x1 -> x0, local copies, waits for them, and re-layouts: 1.62 us -> none
where the time goes in v7:
time: 27.2 us; the launch traced here: 27.1 us
  Pallas kernels  25.4 us (93%)
  other arithmetic  1.69 us (6%)
    pallas_call x1, Pallas kernels, on_device(): pl.pallas_call(functools.partial(kernel, spans, seqs, n, pieces), out_sha...  25.4 us
    convert_element_type x1, other arithmetic, on_device(): return total.astype(bf16)  1.69 us

profile of v7, /device:TPU:21, one launch (start us, length us, event | category | flops | bytes accessed | tf_op | source)
XLA Modules:
  0.0 27.1 jit_solution(4785034447878053303)
XLA Ops:
  0.0 25.4 %shard_map.64 = f32[1,64,1536]{2,1,0:T(8,128)} custom-call(bf16[1,64,1536]{2,1,0:T(8,128)(2,1)} %q_ref.1, bf16[1,64,1024]{2,1,0:T(8,128)(2,1)} %k_ref.1, bf16[1,64,1024]{2,1,0:T(8,128)(2,1)} %v_ref.1, s32[1,64]{1,0:T(1,128)} %bitcast.1, s32[4,4]{1,0:T(4,128)} %mask_ref.1, bf16[1536,6144]{1,0:T(8,128)(2,1)} %w_ref.1), custom_call_target="tpu_custom_call" | custom-call | tf_op jit(solution)/shard_map/pallas_call | solution.py:405
  25.4 1.7 %convert_element_type.3 = bf16[1,64,1536]{2,1,0:T(8,128)(2,1)} convert(f32[1,64,1536]{2,1,0:T(8,128)} %shard_map.64) | non-fusion elementwise | flops 98304 | bytes 589824 | tf_op jit(solution)/shard_map/convert_element_type | solution.py:444

commit v8 on v7

--- a/solution.py
+++ b/solution.py
@@ -17,7 +17,7 @@
 def kernel(
     spans, seqs, n, pieces,
     q_ref, k_ref, v_ref, clip_ref, mask_ref, w_ref, out_ref,
-    qbuf, q_other, kbuf, vbuf, other, own_clip, mask, clips, wbuf, att, part, sendbuf, recvbuf, outbuf,
+    qbuf, q_other, kbuf, vbuf, other, own_clip, mask, clips, wbuf, att, ahead, part, sendbuf, recvbuf, outbuf,
     local_sem, w_sem, q_sem, kv_send, kv_recv, clip_send, clip_recv, sum_send, sum_recv, out_sem,
     att_send, att_recv, out_send, out_recv,
 ):
@@ -257,6 +257,15 @@
             at = (i * att_heads + h) * HEAD_DIM
             att[core, :, at:at + HEAD_DIM] = o[h * 2 * rows:(h + 1) * 2 * rows]
         att_copy(i, core).start()
+    half_depth = my_heads * HEAD_DIM
+
+    def half_product(i, of):
+        depth = pl.ds(pl.multiple_of(of * half_depth, half_depth), half_depth)
+        return jnp.dot(att[of], wbuf[i, depth, :], preferred_element_type=jnp.float32)
+
+    for i in range(2):
+        w_copy(i).wait()
+        ahead[i] = half_product(i, core)
     for i in range(att_parts):
         att_copy(i, 1 - core).wait_recv()
 
@@ -270,13 +279,17 @@
             device_id_type=MESH,
         )
 
-    def project(i):
+    def project(i, begun):
         to, piece = piece_at(i)
         at = to * pieces + piece
-        w_copy(i).wait()
-        product = jnp.dot(
-            jnp.concatenate([att[0], att[1]], axis=1), wbuf[i], preferred_element_type=jnp.float32
-        )
+        if begun:
+            product = ahead[i] + half_product(i, 1 - core)
+        else:
+            w_copy(i).wait()
+            product = jnp.dot(
+                jnp.concatenate([att[0], att[1]], axis=1), wbuf[i],
+                preferred_element_type=jnp.float32,
+            )
         part[at] = product
 
         @pl.when((me == 0) & (to > 0))
@@ -312,8 +325,8 @@
             pass_on(1, down).start()
 
     def project_and_relay(m, carry):
-        project(2 * m)
-        project(2 * m + 1)
+        project(2 * m, False)
+        project(2 * m + 1, False)
         relay_sums(m)
         return carry
 
@@ -321,7 +334,10 @@
         relay_sums(m)
         return carry
 
-    lax.fori_loop(0, steps // 2, project_and_relay, 0)
+    project(0, True)
+    project(1, True)
+    relay_sums(0)
+    lax.fori_loop(1, steps // 2, project_and_relay, 0)
     last = max((n - 1 - z) * pieces + 2 * z - 1 for z in range(1, n))
     lax.fori_loop(steps // 2, last, relay_only, 0)
 
@@ -358,7 +374,7 @@
             pass_on(1, at).wait_recv()
             part[at] += recvbuf[1, at].astype(jnp.float32)
 
-        outbuf[i] = part[at]
+        outbuf[i] = part[at].astype(outbuf.dtype)
         out_to_sibling(i, core).start()
         out_copy(i).start()
 
@@ -388,6 +404,21 @@
         out_copy(i).wait()
         out_to_sibling(i, core).wait_send()
         out_to_sibling(i, 1 - core).wait_recv()
+
+
+def hand_over(x_ref, y_ref, sems):
+    bands = sems.shape[0]
+    height = x_ref.shape[1] // bands
+    copies = [
+        pltpu.make_async_copy(
+            x_ref.at[0, pl.ds(i * height, height)], y_ref.at[0, pl.ds(i * height, height)], sems.at[i]
+        )
+        for i in range(bands)
+    ]
+    for copy in copies:
+        copy.start()
+    for copy in copies:
+        copy.wait()
 
 
 def on_device(queries, keys, values, clip_ids, block_mask, out_weight):
@@ -404,7 +435,7 @@
     hbm = pl.BlockSpec(memory_space=pl.ANY)
     total = pl.pallas_call(
         functools.partial(kernel, spans, seqs, n, pieces),
-        out_shape=jax.ShapeDtypeStruct((1, rows, chunk), jnp.float32),
+        out_shape=jax.ShapeDtypeStruct((1, rows, chunk), bf16),
         in_specs=[hbm] * 6,
         out_specs=hbm,
         scratch_shapes=[
@@ -418,10 +449,11 @@
             pltpu.VMEM((seqs, 8, rows), jnp.int32),
             pltpu.VMEM((n * pieces, depth, width), bf16),
             pltpu.VMEM((2, 2 * rows, local_width // 2), bf16),
+            pltpu.VMEM((2, 2 * rows, width), jnp.float32),
             pltpu.VMEM((n * pieces, 2 * rows, width), jnp.float32),
             pltpu.VMEM((n * pieces, 2 * rows, width), bf16),
             pltpu.VMEM((2, n * pieces, 2 * rows, width), bf16),
-            pltpu.VMEM((pieces, 2 * rows, width), jnp.float32),
+            pltpu.VMEM((pieces, 2 * rows, width), bf16),
             pltpu.SemaphoreType.DMA((8,)),
             pltpu.SemaphoreType.DMA((n * pieces,)),
             pltpu.SemaphoreType.DMA((2,)),
@@ -441,7 +473,14 @@
             collective_id=0, has_side_effects=True, vmem_limit_bytes=64 * 1024 * 1024
         ),
     )(queries, keys, values, clip_ids.reshape(1, rows), block_mask, out_weight)
-    return total.astype(bf16)
+    bands = rows // 16
+    return pl.pallas_call(
+        hand_over,
+        out_shape=jax.ShapeDtypeStruct(total.shape, bf16),
+        in_specs=[hbm],
+        out_specs=hbm,
+        scratch_shapes=[pltpu.SemaphoreType.DMA((bands,))],
+    )(total)
 
 
 def solution(mesh):

time: 27.2 us -> 32.5 us (1.19)
  Pallas kernels: 25.4 us -> 32.3 us
  other arithmetic: 1.69 us -> 0 us
    pallas_call x0 -> x1, Pallas kernels: none -> 7.09 us  [on_device(): pl.pallas_call(hand_over, out_shape=jax.ShapeDtypeStruct(total.shape, bf1...]
    convert_element_type x1 -> x0, other arithmetic: 1.69 us -> none  [on_device(): return total.astype(bf16)]
where the time goes in v8:
time: 32.5 us; the launch traced here: 32.3 us
  Pallas kernels  32.3 us (99%)
    pallas_call x1, Pallas kernels, on_device(): pl.pallas_call(functools.partial(kernel, spans, seqs, n, pieces), out_sha...  25.2 us
    pallas_call x1, Pallas kernels, on_device(): pl.pallas_call(hand_over, out_shape=jax.ShapeDtypeStruct(total.shape, bf1...  7.09 us

profile of v8, /device:TPU:21, one launch (start us, length us, event | category | flops | bytes accessed | tf_op | source)
XLA Modules:
  0.0 32.3 jit_solution(7038871160949796163)
XLA Ops:
  0.0 25.2 %shard_map.64.x_ref = bf16[1,64,1536]{2,1,0:T(8,128)(2,1)} custom-call(bf16[1,64,1536]{2,1,0:T(8,128)(2,1)} %q_ref.1, bf16[1,64,1024]{2,1,0:T(8,128)(2,1)} %k_ref.1, bf16[1,64,1024]{2,1,0:T(8,128)(2,1)} %v_ref.1, s32[1,64]{1,0:T(1,128)} %bitcast.1, s32[4,4]{1,0:T(4,128)} %mask_ref.1, bf16[1536,6144]{1,0:T(8,128)(2,1)} %w_ref.1), custom_call_target="tpu_custom_call" | custom-call | tf_op jit(solution)/shard_map/pallas_call | solution.py:436
  25.2 7.1 %shard_map.65 = bf16[1,64,1536]{2,1,0:T(8,128)(2,1)} custom-call(bf16[1,64,1536]{2,1,0:T(8,128)(2,1)} %shard_map.64.x_ref), custom_call_target="tpu_custom_call" | custom-call | tf_op jit(solution)/shard_map/pallas_call | solution.py:477

commit v9 on v7

--- a/solution.py
+++ b/solution.py
@@ -358,7 +358,7 @@
             pass_on(1, at).wait_recv()
             part[at] += recvbuf[1, at].astype(jnp.float32)
 
-        outbuf[i] = part[at]
+        outbuf[i] = part[at].astype(outbuf.dtype)
         out_to_sibling(i, core).start()
         out_copy(i).start()
 
@@ -402,9 +402,9 @@
     pieces = chunk // 2 // width
     bf16 = jnp.bfloat16
     hbm = pl.BlockSpec(memory_space=pl.ANY)
-    total = pl.pallas_call(
+    return pl.pallas_call(
         functools.partial(kernel, spans, seqs, n, pieces),
-        out_shape=jax.ShapeDtypeStruct((1, rows, chunk), jnp.float32),
+        out_shape=jax.ShapeDtypeStruct((1, rows, chunk), bf16),
         in_specs=[hbm] * 6,
         out_specs=hbm,
         scratch_shapes=[
@@ -421,7 +421,7 @@
             pltpu.VMEM((n * pieces, 2 * rows, width), jnp.float32),
             pltpu.VMEM((n * pieces, 2 * rows, width), bf16),
             pltpu.VMEM((2, n * pieces, 2 * rows, width), bf16),
-            pltpu.VMEM((pieces, 2 * rows, width), jnp.float32),
+            pltpu.VMEM((pieces, 2 * rows, width), bf16),
             pltpu.SemaphoreType.DMA((8,)),
             pltpu.SemaphoreType.DMA((n * pieces,)),
             pltpu.SemaphoreType.DMA((2,)),
@@ -441,7 +441,6 @@
             collective_id=0, has_side_effects=True, vmem_limit_bytes=64 * 1024 * 1024
         ),
     )(queries, keys, values, clip_ids.reshape(1, rows), block_mask, out_weight)
-    return total.astype(bf16)
 
 
 def solution(mesh):

time: 27.2 us -> 27.1 us (level)
  other arithmetic: 1.69 us -> 0 us
  local copies, waits for them, and re-layouts: 0 us -> 1.62 us
    convert_element_type x1 -> x0, other arithmetic: 1.69 us -> none  [on_device(): return total.astype(bf16)]
    unnamed x0 -> x1, local copies, waits for them, and re-layouts: none -> 1.62 us
where the time goes in v9:
time: 27.1 us; the launch traced here: 26.9 us
  Pallas kernels  25.3 us (93%)
  local copies, waits for them, and re-layouts  1.62 us (6%)
    pallas_call x1, Pallas kernels, on_device(): pl.pallas_call(functools.partial(kernel, spans, seqs, n, pieces), out_sha...  25.3 us
    unnamed x1, local copies, waits for them, and re-layouts  1.62 us

profile of v9, /device:TPU:21, one launch (start us, length us, event | category | flops | bytes accessed | tf_op | source)
XLA Modules:
  0.0 26.9 jit_solution(18114145482340374389)
XLA Ops:
  0.0 25.3 %shard_map.64 = bf16[1,64,1536]{2,1,0:T(8,128)(2,1)} custom-call(bf16[1,64,1536]{2,1,0:T(8,128)(2,1)} %q_ref.1, bf16[1,64,1024]{2,1,0:T(8,128)(2,1)} %k_ref.1, bf16[1,64,1024]{2,1,0:T(8,128)(2,1)} %v_ref.1, s32[1,64]{1,0:T(1,128)} %bitcast.1, s32[4,4]{1,0:T(4,128)} %mask_ref.1, bf16[1536,6144]{1,0:T(8,128)(2,1)} %w_ref.1), custom_call_target="tpu_custom_call" | custom-call | tf_op jit(solution)/shard_map/pallas_call | solution.py:405
  25.3 1.6 %copy.8 = bf16[1,64,1536]{2,1,0:T(8,128)(2,1)} copy(bf16[1,64,1536]{2,1,0:T(8,128)(2,1)} %shard_map.64) | data formatting | bytes 393216

commit v10 on v9

--- a/solution.py
+++ b/solution.py
@@ -398,7 +398,7 @@
     assert GROUP % (local_width // HEAD_DIM // 2) == 0
     depth, out_width = out_weight.shape
     chunk = out_width // n
-    width = 256 if chunk % 512 == 0 else HEAD_DIM
+    width = HEAD_DIM
     pieces = chunk // 2 // width
     bf16 = jnp.bfloat16
     hbm = pl.BlockSpec(memory_space=pl.ANY)

time: 27.1 us -> 30.5 us (1.13)
  Pallas kernels: 25.3 us -> 28.7 us
    pallas_call x1, Pallas kernels: 25.3 us -> 28.7 us  [on_device(): pl.pallas_call(functools.partial(kernel, spans, seqs, n, pieces), out_sha...]
where the time goes in v10:
time: 30.5 us; the launch traced here: 30.3 us
  Pallas kernels  28.7 us (94%)
  local copies, waits for them, and re-layouts  1.62 us (5%)
    pallas_call x1, Pallas kernels, on_device(): pl.pallas_call(functools.partial(kernel, spans, seqs, n, pieces), out_sha...  28.7 us
    unnamed x1, local copies, waits for them, and re-layouts  1.62 us

profile of v10, /device:TPU:21, one launch (start us, length us, event | category | flops | bytes accessed | tf_op | source)
XLA Modules:
  0.0 30.3 jit_solution(6849902083032753669)
XLA Ops:
  0.0 28.7 %shard_map.64 = bf16[1,64,1536]{2,1,0:T(8,128)(2,1)} custom-call(bf16[1,64,1536]{2,1,0:T(8,128)(2,1)} %q_ref.1, bf16[1,64,1024]{2,1,0:T(8,128)(2,1)} %k_ref.1, bf16[1,64,1024]{2,1,0:T(8,128)(2,1)} %v_ref.1, s32[1,64]{1,0:T(1,128)} %bitcast.1, s32[4,4]{1,0:T(4,128)} %mask_ref.1, bf16[1536,6144]{1,0:T(8,128)(2,1)} %w_ref.1), custom_call_target="tpu_custom_call" | custom-call | tf_op jit(solution)/shard_map/pallas_call | solution.py:405
  28.7 1.6 %copy.8 = bf16[1,64,1536]{2,1,0:T(8,128)(2,1)} copy(bf16[1,64,1536]{2,1,0:T(8,128)(2,1)} %shard_map.64) | data formatting | bytes 393216
